TPU v7x, 128 devices: a whole 4x4x4 slice. The times are simulated.
128 devices in a mesh: dp: 32 (over x, y, core), mp: 4 (over z).
Axes of the slice: x: 4, y: 4, z: 4, core: 2. Of those that a mesh axis runs over, the one named last changes fastest.
Arguments:
- embeddings: bfloat16 [262144, 2560], P('dp', 'mp')
- centroids: bfloat16 [65536, 2560], P(('dp', 'mp'))
- labels: bfloat16 [65536, 1024], P(('dp', 'mp')), may hold values from -12 to 12
- candidates: int32 [1024, 8], P(('dp', 'mp')), may hold values from 0 to 511, as said below
- counts: int32 [1024], P(('dp', 'mp')), may hold values from 4 to 8, as said below
- home: int32 [512], replicated, may hold values from 0 to 511, as said below
Outputs:
- profiles: bfloat16 [262144, 1024], P(('dp', 'mp'))
Inputs may be any that keep to these rules, and one draw needn't show every extreme that they name: `home`: a permutation of the tiles. `candidates`: candidate tile ids are distinct within a block; entries from position counts[b] on are padding; the candidate tiles of the 8 blocks of one device, padding included, are exactly one tile stored on each device with the same mp index. `counts`: some block of every device has 8.
All inputs are finite; a program needn't handle non-finite values.
Results may differ from a plain program's by a relative error of at most 0.0048.
Values may be sent and summed in bfloat16 or wider, within the bound.
No kernel may reach another device: no remote copies, remote signals or barrier semaphores. Data moves between devices by JAX's collectives and lax.ppermute only.
A program may use at most 192 MiB of HBM per device.

v0:
```python
import math

import jax
import jax.numpy as jnp
from jax import lax
from jax.sharding import PartitionSpec as P

D = 2560
TR = 128
BR = 256
CAND = 8


def body(embeddings, centroids, labels, candidates, counts, home):
    count_dp = lax.axis_size("dp")
    count_mp = lax.axis_size("mp")
    rows = lax.all_to_all(embeddings, "mp", split_axis=0, concat_axis=1, tiled=True)
    width = rows.shape[1]
    label_width = labels.shape[1]
    tile_count = centroids.shape[0] // TR
    tile_total = home.shape[0]
    blocks = candidates.shape[0]
    identity = jnp.arange(tile_total, dtype=jnp.int32)
    storage = jnp.sum(jnp.where(candidates[:, :, None] == identity, home, 0), axis=2)
    owner = storage // tile_count // count_mp
    local = storage % tile_count
    cell = owner * tile_count + local
    table = jnp.arange(count_dp * tile_count, dtype=jnp.int32)
    present = jnp.any(cell.reshape(-1)[:, None] == table[None, :], axis=0).reshape(
        count_dp, tile_count
    )
    wanted = jnp.sum(
        jnp.where(present, jnp.arange(tile_count, dtype=jnp.int32)[None, :], 0), axis=1
    )
    asked = lax.all_to_all(wanted[:, None], "dp", split_axis=0, concat_axis=0, tiled=True)[:, 0]
    stored = jnp.concatenate(
        [centroids.reshape(tile_count, TR, width), labels.reshape(tile_count, TR, label_width)],
        axis=2,
    )
    outgoing = jnp.take(stored, asked, axis=0)
    pool = lax.all_to_all(outgoing, "dp", split_axis=0, concat_axis=0, tiled=True)
    scale = 2.0 / math.sqrt(D)
    block_rows = rows.reshape(blocks, BR, width)

    def score_block(items):
        members, slots, count = items
        chosen = jnp.take(pool, slots, axis=0)
        chosen_cents = chosen[:, :, :width]
        chosen_labels = chosen[:, :, width:]
        logits = (
            jnp.einsum("rd,ctd->rct", members, chosen_cents, preferred_element_type=jnp.float32)
            * scale
        )
        live = (jnp.arange(CAND, dtype=jnp.int32) < count)[None, :, None]
        logits = jnp.where(live, logits, -jnp.inf)
        peak = jnp.max(logits, axis=(1, 2), keepdims=True)
        weights = jnp.exp(logits - peak)
        total = jnp.sum(weights, axis=(1, 2), keepdims=True)
        probs = (weights / total).astype(jnp.bfloat16)
        result = jnp.einsum("rct,ctl->rl", probs, chosen_labels, preferred_element_type=jnp.float32)
        return result.astype(jnp.bfloat16)

    result = lax.map(score_block, (block_rows, owner, counts))
    return result.reshape(blocks * BR, label_width)


def solution(mesh):
    placed = (
        P("dp", "mp"),
        P(("dp", "mp"), None),
        P(("dp", "mp"), None),
        P(("dp", "mp"), None),
        P(("dp", "mp")),
        P(),
    )
    return jax.shard_map(
        body, mesh=mesh, in_specs=placed, out_specs=P(("dp", "mp"), None), check_vma=False
    )
```

profile of v0, /device:TPU:12, one launch (start us, length us, event | category | flops | bytes accessed | tf_op | source)
XLA Modules:
  0.0 810.2 jit_solution(7532229045037352555)
XLA Ops:
  1.5 11.7 %all_to_all.36 = s32[32,1,1]{2,1,0:T(1,128)S(1)} all-to-all(s32[32,1,1]{2,1,0:T(1,128)S(1)} %copy.19), channel_id=1, replica_groups=mesh['dp'=32,'mp'=4] {'dp'}, dimensions={0} | all-to-all | bytes 256 | tf_op jit(solution)/shard_map/all_to_all | solution.py:35
  13.2 6.3 all-to-all-start
  23.5 13.5 %gather_fusion.1 = bf16[32,128,3584]{2,1,0:T(8,128)(2,1)} fusion(bf16[4,128,3584]{2,1,0:T(8,128)(2,1)} %pad_maximum_fusion, s32[1024]{0:T(1024)S(1)} %pad_clamp_fusion.1), kind=kCustom, calls=%fused_computation.1 | custom fusion | bytes 58720384 | tf_op jit(solution)/shard_map/jit(_take)/gather | solution.py:40
  37.0 20.4 %broadcast_select_fusion.1 = bf16[32,128,3584]{2,1,0:T(8,128)(2,1)} fusion(bf16[32,128,3584]{2,1,0:T(8,128)(2,1)} %gather_fusion.1, pred[32]{0:T(512)(128)(4,1)S(1)} %compare_and_fusion.1), kind=kLoop, calls=%fused_computation.28 | loop fusion | flops 14680064 | bytes 58720288 | tf_op jit(solution)/shard_map/jit(_take)/select_n | solution.py:40
  57.4 79.5 %all-to-all-done = bf16[4,2048,640]{2,1,0:T(8,128)(2,1)} async-done(((bf16[4,2048,640]{2,1,0:T(8,128)(2,1)}), bf16[4,2048,640]{2,1,0:T(8,128)(2,1)}, u32[]{:S(2)}, u32[]{:S(2)}) %all-to-all-start) | async-done | bytes 10485792 | tf_op jit(solution)/shard_map/all_to_all | solution.py:17
  136.8 8.3 %all-to-all-start.2 = ((bf16[32,128,3584]{2,1,0:T(8,128)(2,1)}), bf16[32,128,3584]{2,1,0:T(8,128)(2,1)}, u32[]{:S(2)}, u32[]{:S(2)}) async-start(bf16[32,128,3584]{2,1,0:T(8,128)(2,1)} %broadcast_select_fusion.1), calls=%async_computation.2 | async-start | bytes 58720256 | tf_op jit(solution)/shard_map/all_to_all | solution.py:41
  145.2 14.8 %copy.22 = bf16[2048,4,640]{2,1,0:T(4,128)(2,1)} copy(bf16[2048,4,640]{2,0,1:T(8,128)(2,1)} %bitcast.9) | data formatting | bytes 20971520 | tf_op jit(solution)/shard_map/while | solution.py:63
  160.0 17.7 %reshape.183 = bf16[8,256,2560]{2,1,0:T(8,128)(2,1)} reshape(bf16[2048,4,640]{2,1,0:T(4,128)(2,1)} %copy.22) | data formatting | bytes 20971520 | tf_op jit(solution)/shard_map/while | solution.py:63
  177.7 447.0 %all-to-all-done.2 = bf16[32,128,3584]{2,1,0:T(8,128)(2,1)} async-done(((bf16[32,128,3584]{2,1,0:T(8,128)(2,1)}), bf16[32,128,3584]{2,1,0:T(8,128)(2,1)}, u32[]{:S(2)}, u32[]{:S(2)}) %all-to-all-start.2) | async-done | bytes 29360160 | tf_op jit(solution)/shard_map/all_to_all | solution.py:41
  624.8 185.5 %while.10 = (s32[]{:T(128)}, bf16[8,256,1024]{2,1,0:T(8,128)(2,1)}, s32[8]{0:T(128)S(1)}, bf16[8,256,2560]{2,1,0:T(8,128)(2,1)}, s32[8,8]{1,0:T(8,128)S(1)}, /*index=5*/bf16[32,128,3584]{2,1,0:T(8,128)(2,1)}, s32[]{:T(128)}) while((s32[]{:T(128)}, bf16[8,256,1024]{2,1,0:T(8,128)(2,1)}, s32[8]{0:T(128)S(1)}, bf16[8,256,2560]{2,1,0:T(8,128)(2,1)}, ...), condition=%wide.region_6.7_spmd, body=%wide.region_3.6_spmd.sunk | while | flops 1885078144 | bytes 41691932 | solution.py:63
  624.8 13.3 %gather_fusion = bf16[8,128,3584]{2,1,0:T(8,128)(2,1)} fusion(bf16[32,128,3584]{2,1,0:T(8,128)(2,1)} %get-tuple-element.124, s32[1024]{0:T(1024)S(1)} %pad_clamp_fusion.3), kind=kCustom, calls=%fused_computation.clone.1 | custom fusion | bytes 14680096 | tf_op jit(solution)/shard_map/while/body/eval_jaxpr/jit(_take)/gather | solution.py:47
  638.1 3.9 broadcast_select_fusion.3
  648.0 13.3 %gather_fusion = bf16[8,128,3584]{2,1,0:T(8,128)(2,1)} fusion(bf16[32,128,3584]{2,1,0:T(8,128)(2,1)} %get-tuple-element.124, s32[1024]{0:T(1024)S(1)} %pad_clamp_fusion.3), kind=kCustom, calls=%fused_computation.clone.1 | custom fusion | bytes 14680096 | tf_op jit(solution)/shard_map/while/body/eval_jaxpr/jit(_take)/gather | solution.py:47
  661.3 3.9 broadcast_select_fusion.3
  671.2 13.3 %gather_fusion = bf16[8,128,3584]{2,1,0:T(8,128)(2,1)} fusion(bf16[32,128,3584]{2,1,0:T(8,128)(2,1)} %get-tuple-element.124, s32[1024]{0:T(1024)S(1)} %pad_clamp_fusion.3), kind=kCustom, calls=%fused_computation.clone.1 | custom fusion | bytes 14680096 | tf_op jit(solution)/shard_map/while/body/eval_jaxpr/jit(_take)/gather | solution.py:47
  684.5 3.9 broadcast_select_fusion.3
  694.3 13.3 %gather_fusion = bf16[8,128,3584]{2,1,0:T(8,128)(2,1)} fusion(bf16[32,128,3584]{2,1,0:T(8,128)(2,1)} %get-tuple-element.124, s32[1024]{0:T(1024)S(1)} %pad_clamp_fusion.3), kind=kCustom, calls=%fused_computation.clone.1 | custom fusion | bytes 14680096 | tf_op jit(solution)/shard_map/while/body/eval_jaxpr/jit(_take)/gather | solution.py:47
  707.7 3.9 broadcast_select_fusion.3
  717.5 13.3 %gather_fusion = bf16[8,128,3584]{2,1,0:T(8,128)(2,1)} fusion(bf16[32,128,3584]{2,1,0:T(8,128)(2,1)} %get-tuple-element.124, s32[1024]{0:T(1024)S(1)} %pad_clamp_fusion.3), kind=kCustom, calls=%fused_computation.clone.1 | custom fusion | bytes 14680096 | tf_op jit(solution)/shard_map/while/body/eval_jaxpr/jit(_take)/gather | solution.py:47
  740.7 13.3 %gather_fusion = bf16[8,128,3584]{2,1,0:T(8,128)(2,1)} fusion(bf16[32,128,3584]{2,1,0:T(8,128)(2,1)} %get-tuple-element.124, s32[1024]{0:T(1024)S(1)} %pad_clamp_fusion.3), kind=kCustom, calls=%fused_computation.clone.1 | custom fusion | bytes 14680096 | tf_op jit(solution)/shard_map/while/body/eval_jaxpr/jit(_take)/gather | solution.py:47
  763.9 13.3 %gather_fusion = bf16[8,128,3584]{2,1,0:T(8,128)(2,1)} fusion(bf16[32,128,3584]{2,1,0:T(8,128)(2,1)} %get-tuple-element.124, s32[1024]{0:T(1024)S(1)} %pad_clamp_fusion.3), kind=kCustom, calls=%fused_computation.clone.1 | custom fusion | bytes 14680096 | tf_op jit(solution)/shard_map/while/body/eval_jaxpr/jit(_take)/gather | solution.py:47
  777.2 3.9 broadcast_select_fusion.3
  787.1 13.3 %gather_fusion = bf16[8,128,3584]{2,1,0:T(8,128)(2,1)} fusion(bf16[32,128,3584]{2,1,0:T(8,128)(2,1)} %get-tuple-element.124, s32[1024]{0:T(1024)S(1)} %pad_clamp_fusion.3), kind=kCustom, calls=%fused_computation.clone.1 | custom fusion | bytes 14680096 | tf_op jit(solution)/shard_map/while/body/eval_jaxpr/jit(_take)/gather | solution.py:47
  800.4 3.9 broadcast_select_fusion.3
  (84 shorter events, 60.9 us)
Async XLA Ops:
  13.2 6.3 copy-start
  13.2 123.6 %all-to-all-start = ((bf16[4,2048,640]{2,1,0:T(8,128)(2,1)}), bf16[4,2048,640]{2,1,0:T(8,128)(2,1)}, u32[]{:S(2)}, u32[]{:S(2)}) async-start(bf16[4,2048,640]{2,1,0:T(8,128)(2,1)} %bitcast.51), calls=%async_computation | async-start | bytes 20971520 | tf_op jit(solution)/shard_map/all_to_all | solution.py:17
  136.8 487.9 %all-to-all-start.2 = ((bf16[32,128,3584]{2,1,0:T(8,128)(2,1)}), bf16[32,128,3584]{2,1,0:T(8,128)(2,1)}, u32[]{:S(2)}, u32[]{:S(2)}) async-start(bf16[32,128,3584]{2,1,0:T(8,128)(2,1)} %broadcast_select_fusion.1), calls=%async_computation.2 | async-start | bytes 58720256 | tf_op jit(solution)/shard_map/all_to_all | solution.py:41
  160.0 464.7 %copy-start.1 = (s32[8]{0:T(128)S(1)}, s32[8]{0:T(128)}, u32[]{:S(2)}) copy-start(s32[8]{0:T(128)} %param.12) | copy-start | bytes 100
where the time goes:
time: 812 us; the launch traced here: 810 us
  waiting for transfers between devices  527 us (65%)
  local copies, waits for them, and re-layouts  158 us (19%)
  other arithmetic  63.4 us (8%)
  matrix products  35.6 us (4%)
  starting transfers between devices  14.6 us (2%)
  blocking collectives  11.7 us (1%)
    all_to_all x1, waiting for transfers between devices, body(): lax.all_to_all(outgoing, 'dp', split_axis=0, concat_axis=0, tiled=True)  447 us
    gather x8, local copies, waits for them, and re-layouts, score_block(): chosen = jnp.take(pool, slots, axis=0)  107 us
    all_to_all x1, waiting for transfers between devices, body(): lax.all_to_all(embeddings, 'mp', split_axis=0, concat_axis=1, tiled=True)  79.5 us
    while x2, local copies, waits for them, and re-layouts, body(): result = lax.map(score_block, (block_rows, owner, counts))  32.5 us
    select_n x16, other arithmetic, score_block(): chosen = jnp.take(pool, slots, axis=0)  30.9 us
    dot_general x8, matrix products, score_block(): jnp.einsum('rd,ctd->rct', members, chosen_cents, preferred_element_type=j...  23.1 us
    select_n x2, other arithmetic, body(): outgoing = jnp.take(stored, asked, axis=0)  20.4 us
  transfers between devices with their start and end apart: 2, of which 2 were waited for; matrix products, arithmetic and copies ran while one was open for 9% of the time, Pallas kernels for 0%

commit v1 on v0

v1 whole, which is shorter than its diff:
```python
import functools
import math

import jax
import jax.numpy as jnp
from jax import lax
from jax.experimental import pallas as pl
from jax.experimental.pallas import tpu as pltpu
from jax.sharding import PartitionSpec as P

D = 2560
LAB = 1024
TR = 128
HR = TR // 2
BR = 256
CAND = 8
NX = 4
NY = 4
NC = 2
NZ = 4
NDP = NX * NY * NC
TILE_DEV = 4
BLK_DEV = 8
WIDE = D + LAB
PIECE = D // NZ
ROWS = BLK_DEV * BR
HBM = pl.BlockSpec(memory_space=pl.ANY)
SMEM = pl.BlockSpec(memory_space=pltpu.SMEM)


def dp_index(x, y, c):
    return ((x % NX) * NY + (y % NY)) * NC + c


def shift(value, dx, dy, flip):
    pairs = [
        (dp_index(x, y, c), dp_index(x + dx, y + dy, c ^ flip))
        for x in range(NX)
        for y in range(NY)
        for c in range(NC)
    ]
    return lax.ppermute(value, "dp", pairs)


def pick_kernel(targets, table, place, *refs):
    held = (refs[0:5], refs[5:10])
    outs = refs[10:-1]
    sem = refs[-1]
    x, y, c = place[0], place[1], place[2]
    count = 0
    for side in range(2):
        own, before, after, low, high = held[side]
        for step, flip in targets:
            out = outs[count // 4]
            for r in range(4):
                if side == 0:
                    target = (x * NY + ((y + step) & 3)) * NC + (c ^ flip)
                    owner = (((x + r) & 3) * NY + y) * NC + c
                else:
                    target = (((x + step) & 3) * NY + y) * NC + (c ^ flip)
                    owner = (x * NY + ((y + r) & 3)) * NC + c
                w = table[target, owner]
                if r == 2:

                    @pl.when(w < 2)
                    def _():
                        pltpu.make_async_copy(low.at[jnp.minimum(w, 1)], out.at[r], sem.at[count]).start()

                    @pl.when(w >= 2)
                    def _():
                        pltpu.make_async_copy(high.at[jnp.maximum(w - 2, 0)], out.at[r], sem.at[count]).start()
                else:
                    source = (own, after, None, before)[r]
                    pltpu.make_async_copy(source.at[w], out.at[r], sem.at[count]).start()
                count += 1
    for i in range(count):
        pltpu.make_async_copy(held[0][0].at[0], outs[i // 4].at[i % 4], sem.at[i]).wait()


def pick(targets, table, place, held):
    sends = 2 * len(targets)
    shape = jax.ShapeDtypeStruct((4, HR, WIDE), jnp.bfloat16)
    size = sends * 4 * HR * WIDE * 2
    return pl.pallas_call(
        functools.partial(pick_kernel, targets),
        out_shape=[shape] * sends,
        in_specs=[SMEM, SMEM] + [HBM] * 10,
        out_specs=[HBM] * sends,
        scratch_shapes=[pltpu.SemaphoreType.DMA((sends * 4,))],
        cost_estimate=pl.CostEstimate(flops=0, bytes_accessed=2 * size, transcendentals=0),
    )(table, place, *held)


def score_kernel(owners, fresh, counts, place, *refs):
    got = (refs[0:8], refs[8:16])
    parts = refs[16:20]
    out = refs[20]
    cents, labs, rows, logits, tile_sem, row_sem = refs[21:]
    b = pl.program_id(0)
    x, y, c, z = place[0], place[1], place[2], place[3]

    def tile_copies(side, k, r, o):
        source = got[side][k]
        half = pl.ds(side * HR, HR)
        return (
            pltpu.make_async_copy(
                source.at[r, :, pl.ds(0, D)], cents.at[o, half, :], tile_sem.at[2 * side, o]
            ),
            pltpu.make_async_copy(
                source.at[r, :, pl.ds(D, LAB)], labs.at[o, half, :], tile_sem.at[2 * side + 1, o]
            ),
        )

    def fetch(block):
        def one(j, carry):
            at = block * CAND + j

            @pl.when(fresh[at] > 0)
            def _():
                o = owners[at]
                rx = ((o >> 3) - x) & 3
                ry = ((o >> 1) - y) & 3
                rc = (o & 1) ^ c
                for side, near, r in ((0, ry, rx), (1, rx, ry)):
                    which = near * 2 + rc
                    for k in range(8):

                        @pl.when(which == k)
                        def _():
                            for copy in tile_copies(side, k, r, o):
                                copy.start()

            return carry

        lax.fori_loop(0, CAND, one, 0)

    def row_copies(block):
        slot = lax.rem(block, 2)
        for r in range(NZ):
            start = block * BR + (z * ROWS if r == 0 else 0)
            column = pl.multiple_of(((z + r) & 3) * PIECE, 128)
            yield pltpu.make_async_copy(
                parts[r].at[pl.ds(pl.multiple_of(start, BR), BR), :],
                rows.at[slot, :, pl.ds(column, PIECE)],
                row_sem.at[slot, r],
            )

    @pl.when(b == 0)
    def _():
        for copy in row_copies(b):
            copy.start()
        fetch(b)

    @pl.when(b + 1 < BLK_DEV)
    def _():
        for copy in row_copies(b + 1):
            copy.start()
        fetch(b + 1)

    for copy in row_copies(b):
        copy.wait()

    def settle(j, carry):
        at = b * CAND + j

        @pl.when(fresh[at] > 0)
        def _():
            o = owners[at]
            for side in range(2):
                for copy in tile_copies(side, 0, 0, o):
                    copy.wait()

        return carry

    lax.fori_loop(0, CAND, settle, 0)

    live = counts[b]
    members = rows.at[lax.rem(b, 2)]
    scale = 2.0 / math.sqrt(D)
    for pair in range(CAND // 2):
        columns = slice(pair * 2 * TR, (pair + 1) * 2 * TR)

        @pl.when(2 * pair < live)
        def _():
            first = owners[b * CAND + 2 * pair]
            second = owners[b * CAND + 2 * pair + 1]
            tiles = jnp.concatenate([cents[first], cents[second]], axis=0)
            value = lax.dot_general(
                members[...], tiles, (((1,), (1,)), ((), ())), preferred_element_type=jnp.float32
            )
            column = lax.broadcasted_iota(jnp.int32, (BR, 2 * TR), 1) + pair * 2 * TR
            logits[:, columns] = jnp.where(column < live * TR, value * scale, -jnp.inf)

        @pl.when(2 * pair >= live)
        def _():
            logits[:, columns] = jnp.full((BR, 2 * TR), -jnp.inf, jnp.float32)

    value = logits[...]
    peak = jnp.max(value, axis=1, keepdims=True)
    weights = jnp.exp(value - peak)
    total = jnp.sum(weights, axis=1, keepdims=True)
    probs = (weights / total).astype(jnp.bfloat16)
    tiles = jnp.concatenate([labs[owners[b * CAND + j]] for j in range(CAND)], axis=0)
    result = jnp.dot(probs, tiles, preferred_element_type=jnp.float32)
    out[...] = result.astype(jnp.bfloat16)


def score(owners, fresh, counts, place, got, parts):
    return pl.pallas_call(
        score_kernel,
        out_shape=jax.ShapeDtypeStruct((ROWS, LAB), jnp.bfloat16),
        grid_spec=pltpu.PrefetchScalarGridSpec(
            num_scalar_prefetch=4,
            grid=(BLK_DEV,),
            in_specs=[HBM] * 20,
            out_specs=pl.BlockSpec((BR, LAB), lambda b, *_: (b, 0)),
            scratch_shapes=[
                pltpu.VMEM((NDP, TR, D), jnp.bfloat16),
                pltpu.VMEM((NDP, TR, LAB), jnp.bfloat16),
                pltpu.VMEM((2, BR, D), jnp.bfloat16),
                pltpu.VMEM((BR, CAND * TR), jnp.float32),
                pltpu.SemaphoreType.DMA((4, NDP)),
                pltpu.SemaphoreType.DMA((2, NZ)),
            ],
        ),
        compiler_params=pltpu.CompilerParams(
            dimension_semantics=("arbitrary",), vmem_limit_bytes=56 * 1024 * 1024
        ),
        cost_estimate=pl.CostEstimate(
            flops=2 * ROWS * CAND * TR * WIDE,
            bytes_accessed=NDP * TR * WIDE * 2 + ROWS * WIDE * 2,
            transcendentals=ROWS * CAND * TR,
        ),
    )(owners, fresh, counts, place, *got, *parts)


def body(embeddings, centroids, labels, candidates, counts, home):
    me = lax.axis_index("dp")
    z = lax.axis_index("mp")
    place = jnp.stack([me // (NY * NC), (me // NC) % NY, me % NC, z]).astype(jnp.int32)

    tiles = centroids.reshape(TILE_DEV, TR, D)
    tile_labels = labels.reshape(TILE_DEV, TR, LAB)
    own = [
        jnp.concatenate([tiles[:, s : s + HR], tile_labels[:, s : s + HR]], axis=2) for s in (0, HR)
    ]
    held = []
    for side in range(2):
        dx, dy = ((1, 0), (0, 1))[side]
        before = shift(own[side], dx, dy, 0)
        after = shift(own[side], -dx, -dy, 0)
        low = shift(before[:2], dx, dy, 0)
        high = shift(after[2:], -dx, -dy, 0)
        held += [own[side], before, after, low, high]

    identity = jnp.arange(home.shape[0], dtype=jnp.int32)
    storage = jnp.sum(jnp.where(candidates[:, :, None] == identity, home, 0), axis=2)
    owner = storage // (TILE_DEV * NZ)
    local = storage % TILE_DEV
    hit = owner.reshape(-1)[:, None] == jnp.arange(NDP, dtype=jnp.int32)[None, :]
    wanted = jnp.max(jnp.where(hit, local.reshape(-1)[:, None], 0), axis=0)
    table = lax.all_gather(wanted, "dp")

    parts = [embeddings]
    for r in range(1, NZ):
        target = (z - r) % NZ
        piece = lax.dynamic_slice_in_dim(embeddings, target * ROWS, ROWS, 0)
        parts.append(lax.ppermute(piece, "mp", [(i, (i - r) % NZ) for i in range(NZ)]))

    got = [[None] * 8, [None] * 8]
    for targets in (((1, 0), (3, 0)), ((1, 1), (3, 1)), ((2, 0), (2, 1)), ((0, 0), (0, 1))):
        sends = pick(targets, table, place, held)
        for side in range(2):
            for i, (step, flip) in enumerate(targets):
                value = sends[side * len(targets) + i]
                if (step, flip) != (0, 0):
                    value = shift(value, step * side, step * (1 - side), flip)
                got[side][((-step) % 4) * 2 + flip] = value

    live = jnp.arange(CAND, dtype=jnp.int32)[None, :] < counts[:, None]
    slots = jnp.where(live, owner, owner[:, :1])
    flat = slots.reshape(-1)
    order = jnp.arange(BLK_DEV * CAND, dtype=jnp.int32) // CAND
    seen = (flat[:, None] == flat[None, :]) & (order[None, :] < order[:, None])
    fresh = (live.reshape(-1) & ~jnp.any(seen, axis=1)).astype(jnp.int32)
    return score(flat, fresh, counts, place, got[0] + got[1], parts)


def solution(mesh):
    placed = (
        P("dp", "mp"),
        P(("dp", "mp"), None),
        P(("dp", "mp"), None),
        P(("dp", "mp"), None),
        P(("dp", "mp")),
        P(),
    )
    return jax.shard_map(
        body, mesh=mesh, in_specs=placed, out_specs=P(("dp", "mp"), None), check_vma=False
    )
```

time: 812 us -> 1100 us (1.35)
  Pallas kernels: 0 us -> 928 us
  waiting for transfers between devices: 527 us -> 78.5 us
  local copies, waits for them, and re-layouts: 158 us -> 21.9 us
  other arithmetic: 63.4 us -> 3.41 us
  matrix products: 35.6 us -> 0 us
  starting transfers between devices: 14.6 us -> 36.9 us
    pallas_call x0 -> x5, Pallas kernels: none -> 928 us  [the longest x4 898 us: pick(): pl.pallas_call(functools.partial(pick_kernel, targets), out_shape=[shape]...]
    all_to_all x2 -> x0, waiting for transfers between devices: 527 us -> none  [the longest x1 447 us: body(): lax.all_to_all(outgoing, 'dp', split_axis=0, concat_axis=0, tiled=True)]
    gather x9 -> x0, local copies, waits for them, and re-layouts: 120 us -> none  [the longest x8 107 us: score_block(): chosen = jnp.take(pool, slots, axis=0)]
    ppermute x0 -> x25, waiting for transfers between devices: none -> 78.5 us  [the longest x22 78.5 us: shift(): return lax.ppermute(value, 'dp', pairs)]
    select_n x19 -> x3, other arithmetic: 51.3 us -> 0.02 us  [the longest x1 0.01 us: body(): slots = jnp.where(live, owner, owner[:, :1])]
    ppermute x0 -> x25, starting transfers between devices: none -> 36.9 us  [the longest x22 28 us: shift(): return lax.ppermute(value, 'dp', pairs)]
    dot_general x16 -> x0, matrix products: 35.6 us -> none  [the longest x8 23.1 us: score_block(): jnp.einsum('rd,ctd->rct', members, chosen_cents, preferred_element_type=j...]
    while x2 -> x0, local copies, waits for them, and re-layouts: 32.5 us -> none  [body(): result = lax.map(score_block, (block_rows, owner, counts))]
  transfers between devices with their start and end apart: 2 -> 25, of which waited for: 2 -> 5; matrix products, arithmetic and copies ran while one was open for 9% -> 2% of each run, Pallas kernels for 0% -> 82%
where the time goes in v1:
time: 1100 us; the launch traced here: 1090 us
  Pallas kernels  928 us (84%)
  waiting for transfers between devices  78.5 us (7%)
  starting transfers between devices  36.9 us (3%)
  local copies, waits for them, and re-layouts  21.9 us (2%)
  blocking collectives  20.4 us (2%)
    pallas_call x4, Pallas kernels, pick(): pl.pallas_call(functools.partial(pick_kernel, targets), out_shape=[shape]...  898 us
    ppermute x22, waiting for transfers between devices, shift(): return lax.ppermute(value, 'dp', pairs)  78.5 us
    pallas_call x1, Pallas kernels, score(): pl.pallas_call(score_kernel, out_shape=jax.ShapeDtypeStruct((ROWS, LAB),...  30.2 us
    ppermute x22, starting transfers between devices, shift(): return lax.ppermute(value, 'dp', pairs)  28 us
  transfers between devices with their start and end apart: 25, of which 5 were waited for; matrix products, arithmetic and copies ran while one was open for 2% of the time, Pallas kernels for 82%

profile of v1, /device:TPU:12, one launch (start us, length us, event | category | flops | bytes accessed | tf_op | source)
XLA Modules:
  0.0 1090.5 jit_solution(5784131509826081445)
XLA Ops:
  0.0 2.0 fusion.3
  7.7 6.8 constant_dynamic-slice_fusion
  14.5 4.0 collective-permute-start.22
  18.6 25.6 %collective-permute-done.refs_1_ = bf16[4,64,3584]{2,1,0:T(8,128)(2,1)} collective-permute-done((bf16[4,64,3584]{2,1,0:T(8,128)(2,1)S(1)}, bf16[4,64,3584]{2,1,0:T(8,128)(2,1)}, u32[]{:S(2)}, u32[]{:S(2)}) %collective-permute-start) | collective-permute-done | bytes 1835040 | tf_op jit(solution)/shard_map/ppermute | solution.py:42
  44.2 3.9 collective-permute-start.23
  48.0 2.2 slice.38
  51.4 2.2 slice.39
  54.8 2.2 slice.42
  58.6 2.2 slice.43
  60.8 10.6 collective-permute-done.2.refs_3_
  71.8 2.7 collective-permute-done.3.refs_4_
  77.7 20.4 %all-reduce = s32[1024]{0:T(1024)S(1)} all-reduce(s32[1024]{0:T(1024)S(1)} %dynamic-update-slice), channel_id=2, replica_groups=mesh['dp'=32,'mp'=4] {'dp'}, use_global_device_ids=true, to_apply=%add | all-reduce | flops 1024 | bytes 8192
  100.4 224.5 %shard_map.67 = (bf16[4,64,3584]{2,1,0:T(8,128)(2,1)}, bf16[4,64,3584]{2,1,0:T(8,128)(2,1)}, bf16[4,64,3584]{2,1,0:T(8,128)(2,1)}, bf16[4,64,3584]{2,1,0:T(8,128)(2,1)}) custom-call(s32[32,32]{1,0:T(8,128)} %reshape.171.table, s32[4]{0:T(128)} %pad_add_fusion.place, bf16[4,64,3584]{2,1,0:T(8,128)(2,1)} %copy-done, ...), custom_call_target="tpu_custom_call" | custom-call | bytes 14680064 | tf_op jit(solution)/shard_map/pallas_call | solution.py:84
  326.0 2.7 collective-permute-start.18
  328.8 2.7 collective-permute-start.19
  331.5 224.5 %shard_map.66 = (bf16[4,64,3584]{2,1,0:T(8,128)(2,1)}, bf16[4,64,3584]{2,1,0:T(8,128)(2,1)}, bf16[4,64,3584]{2,1,0:T(8,128)(2,1)}, bf16[4,64,3584]{2,1,0:T(8,128)(2,1)}) custom-call(s32[32,32]{1,0:T(8,128)} %reshape.171.table, s32[4]{0:T(128)} %pad_add_fusion.place, bf16[4,64,3584]{2,1,0:T(8,128)(2,1)} %copy-done, ...), custom_call_target="tpu_custom_call" | custom-call | bytes 14680064 | tf_op jit(solution)/shard_map/pallas_call | solution.py:84
  556.0 224.6 %shard_map.65 = (bf16[4,64,3584]{2,1,0:T(8,128)(2,1)}, bf16[4,64,3584]{2,1,0:T(8,128)(2,1)}, bf16[4,64,3584]{2,1,0:T(8,128)(2,1)}, bf16[4,64,3584]{2,1,0:T(8,128)(2,1)}) custom-call(s32[32,32]{1,0:T(8,128)} %reshape.171.table, s32[4]{0:T(128)} %pad_add_fusion.place, bf16[4,64,3584]{2,1,0:T(8,128)(2,1)} %copy-done, ...), custom_call_target="tpu_custom_call" | custom-call | bytes 14680064 | tf_op jit(solution)/shard_map/pallas_call | solution.py:84
  780.6 3.5 collective-permute-start.10
  784.1 2.4 collective-permute-start.17
  788.5 224.5 %shard_map.64 = (bf16[4,64,3584]{2,1,0:T(8,128)(2,1)}, bf16[4,64,3584]{2,1,0:T(8,128)(2,1)}, bf16[4,64,3584]{2,1,0:T(8,128)(2,1)}, bf16[4,64,3584]{2,1,0:T(8,128)(2,1)}) custom-call(s32[32,32]{1,0:T(8,128)} %reshape.171.table, s32[4]{0:T(128)} %pad_add_fusion.place, bf16[4,64,3584]{2,1,0:T(8,128)(2,1)} %copy-done, ...), custom_call_target="tpu_custom_call" | custom-call | bytes 14680064 | tf_op jit(solution)/shard_map/pallas_call | solution.py:84
  1013.2 3.0 collective-permute-start.20
  1019.2 37.4 %collective-permute-done.16.refs_10_ = bf16[4,64,3584]{2,1,0:T(8,128)(2,1)S(1)} collective-permute-done((bf16[4,64,3584]{2,1,0:T(8,128)(2,1)}, bf16[4,64,3584]{2,1,0:T(8,128)(2,1)S(1)}, u32[]{:S(2)}, u32[]{:S(2)}) %collective-permute-start.16) | collective-permute-done | bytes 1835040 | tf_op jit(solution)/shard_map/ppermute | solution.py:42
  1056.7 2.2 collective-permute-done.9.refs_2_
  1060.1 30.2 %shard_map.68 = bf16[2048,1024]{1,0:T(8,128)(2,1)} custom-call(s32[64]{0:T(128)} %copy-done.5, s32[64]{0:T(128)} %and_convert_fusion.fresh, s32[8]{0:T(128)} %counts.1, s32[4]{0:T(128)} %pad_add_fusion.place, bf16[4,64,3584]{2,1,0:T(8,128)(2,1)} %get-tuple-element.21.refs_0_, bf16[4,64,3584]{2,1,0:T(8,128)(2,1)} %collective-permute-done.8.refs_1_, ...), custom_call_target="tpu_custom_call" | custom-call | flops 15032385536 | bytes 44040192 | tf_op jit(solution)/shard_map/pallas_call | solution.py:209
  (87 shorter events, 22.4 us)
Async XLA Ops:
  2.2 41.9 %collective-permute-start = (bf16[4,64,3584]{2,1,0:T(8,128)(2,1)S(1)}, bf16[4,64,3584]{2,1,0:T(8,128)(2,1)}, u32[]{:S(2)}, u32[]{:S(2)}) collective-permute-start(bf16[4,64,3584]{2,1,0:T(8,128)(2,1)S(1)} %pad_maximum_fusion.refs_0_), channel_id=1, source_target_pairs={{0,32},{4,36},{8,40},{12,44},{16,48},{20,52},{24,56},{28,60},{32,6... | collective-permute-start | bytes 5505032 | tf_op jit(solution)/shard_map/ppermute | solution.py:42
  3.5 46.7 %collective-permute-start.1 = (bf16[4,64,3584]{2,1,0:T(8,128)(2,1)S(1)}, bf16[4,64,3584]{2,1,0:T(8,128)(2,1)}, u32[]{:S(2)}, u32[]{:S(2)}) collective-permute-start(bf16[4,64,3584]{2,1,0:T(8,128)(2,1)S(1)} %pad_maximum_fusion.refs_0_), channel_id=1, source_target_pairs={{0,96},{4,100},{8,104},{12,108},{16,112},{20,116},{24,120},{28,124... | collective-permute-start | bytes 5505032 | tf_op jit(solution)/shard_map/ppermute | solution.py:42
  5.7 47.9 %collective-permute-start.4 = (bf16[4,64,3584]{2,1,0:T(8,128)(2,1)}, bf16[4,64,3584]{2,1,0:T(8,128)(2,1)}, u32[]{:S(2)}, u32[]{:S(2)}) collective-permute-start(bf16[4,64,3584]{2,1,0:T(8,128)(2,1)} %pad_maximum_fusion.1.refs_5_), channel_id=1, source_target_pairs={{0,8},{4,12},{8,16},{12,20},{16,24},{20,28},{24,0},{28,4},{32,40},... | collective-permute-start | bytes 5505032 | tf_op jit(solution)/shard_map/ppermute | solution.py:42
  7.3 49.8 %collective-permute-start.5 = (bf16[4,64,3584]{2,1,0:T(8,128)(2,1)}, bf16[4,64,3584]{2,1,0:T(8,128)(2,1)}, u32[]{:S(2)}, u32[]{:S(2)}) collective-permute-start(bf16[4,64,3584]{2,1,0:T(8,128)(2,1)} %pad_maximum_fusion.1.refs_5_), channel_id=1, source_target_pairs={{0,24},{4,28},{8,0},{12,4},{16,8},{20,12},{24,16},{28,20},{32,56},... | collective-permute-start | bytes 5505032 | tf_op jit(solution)/shard_map/ppermute | solution.py:42
  14.5 311.5 %collective-permute-start.22 = (bf16[2048,640]{1,0:T(8,128)(2,1)}, bf16[2048,640]{1,0:T(8,128)(2,1)}, u32[]{:S(2)}, u32[]{:S(2)}) collective-permute-start(bf16[2048,640]{1,0:T(8,128)(2,1)} %get-tuple-element.41), channel_id=1, source_target_pairs={{0,3},{1,0},{2,1},{3,2},{4,7},{5,4},{6,5},{7,6},{8,11},{9,8},{10,9... | collective-permute-start | bytes 7864328 | tf_op jit(solution)/shard_map/ppermute | solution.py:268
  44.2 284.6 %collective-permute-start.23 = (bf16[2048,640]{1,0:T(8,128)(2,1)}, bf16[2048,640]{1,0:T(8,128)(2,1)}, u32[]{:S(2)}, u32[]{:S(2)}) collective-permute-start(bf16[2048,640]{1,0:T(8,128)(2,1)} %get-tuple-element.40), channel_id=1, source_target_pairs={{0,2},{1,3},{2,0},{3,1},{4,6},{5,7},{6,4},{7,5},{8,10},{9,11},{10,... | collective-permute-start | bytes 7864328 | tf_op jit(solution)/shard_map/ppermute | solution.py:268
  50.2 21.1 %collective-permute-start.2 = (bf16[2,64,3584]{2,1,0:T(8,128)(2,1)}, bf16[2,64,3584]{2,1,0:T(8,128)(2,1)S(1)}, u32[]{:S(2)}, u32[]{:S(2)}) collective-permute-start(bf16[2,64,3584]{2,1,0:T(8,128)(2,1)} %slice.38), channel_id=1, source_target_pairs={{0,32},{4,36},{8,40},{12,44},{16,48},{20,52},{24,56},{28,60},{32,6... | collective-permute-start | bytes 2752520 | tf_op jit(solution)/shard_map/ppermute | solution.py:42
  57.0 42.4 %collective-permute-start.6 = (bf16[2,64,3584]{2,1,0:T(8,128)(2,1)}, bf16[2,64,3584]{2,1,0:T(8,128)(2,1)S(1)}, u32[]{:S(2)}, u32[]{:S(2)}) collective-permute-start(bf16[2,64,3584]{2,1,0:T(8,128)(2,1)} %slice.42), channel_id=1, source_target_pairs={{0,8},{4,12},{8,16},{12,20},{16,24},{20,28},{24,0},{28,4},{32,40},... | collective-permute-start | bytes 2752520 | tf_op jit(solution)/shard_map/ppermute | solution.py:42
  71.4 28.0 %collective-permute-start.7 = (bf16[2,64,3584]{2,1,0:T(8,128)(2,1)}, bf16[2,64,3584]{2,1,0:T(8,128)(2,1)}, u32[]{:S(2)}, u32[]{:S(2)}) collective-permute-start(bf16[2,64,3584]{2,1,0:T(8,128)(2,1)} %slice.43), channel_id=1, source_target_pairs={{0,24},{4,28},{8,0},{12,4},{16,8},{20,12},{24,16},{28,20},{32,56},... | collective-permute-start | bytes 2752520 | tf_op jit(solution)/shard_map/ppermute | solution.py:42
  74.5 706.1 %collective-permute-start.24 = (bf16[2048,640]{1,0:T(8,128)(2,1)}, bf16[2048,640]{1,0:T(8,128)(2,1)}, u32[]{:S(2)}, u32[]{:S(2)}) collective-permute-start(bf16[2048,640]{1,0:T(8,128)(2,1)} %get-tuple-element.39), channel_id=1, source_target_pairs={{0,1},{1,2},{2,3},{3,0},{4,5},{5,6},{6,7},{7,4},{8,9},{9,10},{10,1... | collective-permute-start | bytes 7864328 | tf_op jit(solution)/shard_map/ppermute | solution.py:268
  324.9 459.2 %collective-permute-start.11 = (bf16[4,64,3584]{2,1,0:T(8,128)(2,1)}, bf16[4,64,3584]{2,1,0:T(8,128)(2,1)S(1)}, u32[]{:S(2)}, u32[]{:S(2)}) collective-permute-start(bf16[4,64,3584]{2,1,0:T(8,128)(2,1)} %get-tuple-element.25), channel_id=1, source_target_pairs={{0,16},{4,20},{8,24},{12,28},{16,0},{20,4},{24,8},{28,12},{32,48},... | collective-permute-start | bytes 5505032 | tf_op jit(solution)/shard_map/ppermute | solution.py:42
  326.0 458.1 %collective-permute-start.12 = (bf16[4,64,3584]{2,1,0:T(8,128)(2,1)}, bf16[4,64,3584]{2,1,0:T(8,128)(2,1)}, u32[]{:S(2)}, u32[]{:S(2)}) collective-permute-start(bf16[4,64,3584]{2,1,0:T(8,128)(2,1)} %get-tuple-element.26), channel_id=1, source_target_pairs={{0,20},{4,16},{8,28},{12,24},{16,4},{20,0},{24,12},{28,8},{32,52},... | collective-permute-start | bytes 5505032 | tf_op jit(solution)/shard_map/ppermute | solution.py:42
  326.0 460.5 %collective-permute-start.18 = (bf16[4,64,3584]{2,1,0:T(8,128)(2,1)}, bf16[4,64,3584]{2,1,0:T(8,128)(2,1)}, u32[]{:S(2)}, u32[]{:S(2)}) collective-permute-start(bf16[4,64,3584]{2,1,0:T(8,128)(2,1)} %get-tuple-element.33), channel_id=1, source_target_pairs={{0,64},{4,68},{8,72},{12,76},{16,80},{20,84},{24,88},{28,92},{32,9... | collective-permute-start | bytes 5505032 | tf_op jit(solution)/shard_map/ppermute | solution.py:42
  328.8 459.6 %collective-permute-start.19 = (bf16[4,64,3584]{2,1,0:T(8,128)(2,1)}, bf16[4,64,3584]{2,1,0:T(8,128)(2,1)}, u32[]{:S(2)}, u32[]{:S(2)}) collective-permute-start(bf16[4,64,3584]{2,1,0:T(8,128)(2,1)} %get-tuple-element.34), channel_id=1, source_target_pairs={{0,68},{4,64},{8,76},{12,72},{16,84},{20,80},{24,92},{28,88},{32,1... | collective-permute-start | bytes 5505032 | tf_op jit(solution)/shard_map/ppermute | solution.py:42
  780.6 232.5 %collective-permute-start.10 = (bf16[4,64,3584]{2,1,0:T(8,128)(2,1)}, bf16[4,64,3584]{2,1,0:T(8,128)(2,1)}, u32[]{:S(2)}, u32[]{:S(2)}) collective-permute-start(bf16[4,64,3584]{2,1,0:T(8,128)(2,1)} %get-tuple-element.24), channel_id=1, source_target_pairs={{0,28},{4,24},{8,4},{12,0},{16,12},{20,8},{24,20},{28,16},{32,60},... | collective-permute-start | bytes 5505032 | tf_op jit(solution)/shard_map/ppermute | solution.py:42
  784.1 229.1 %collective-permute-start.14 = (bf16[4,64,3584]{2,1,0:T(8,128)(2,1)}, bf16[4,64,3584]{2,1,0:T(8,128)(2,1)}, u32[]{:S(2)}, u32[]{:S(2)}) collective-permute-start(bf16[4,64,3584]{2,1,0:T(8,128)(2,1)} %get-tuple-element.28), channel_id=1, source_target_pairs={{0,12},{4,8},{8,20},{12,16},{16,28},{20,24},{24,4},{28,0},{32,44},... | collective-permute-start | bytes 5505032 | tf_op jit(solution)/shard_map/ppermute | solution.py:42
  784.1 232.1 %collective-permute-start.17 = (bf16[4,64,3584]{2,1,0:T(8,128)(2,1)}, bf16[4,64,3584]{2,1,0:T(8,128)(2,1)}, u32[]{:S(2)}, u32[]{:S(2)}) collective-permute-start(bf16[4,64,3584]{2,1,0:T(8,128)(2,1)} %get-tuple-element.32), channel_id=1, source_target_pairs={{0,100},{4,96},{8,108},{12,104},{16,116},{20,112},{24,124},{28,120... | collective-permute-start | bytes 5505032 | tf_op jit(solution)/shard_map/ppermute | solution.py:42
  786.6 231.3 %collective-permute-start.21 = (bf16[4,64,3584]{2,1,0:T(8,128)(2,1)}, bf16[4,64,3584]{2,1,0:T(8,128)(2,1)}, u32[]{:S(2)}, u32[]{:S(2)}) collective-permute-start(bf16[4,64,3584]{2,1,0:T(8,128)(2,1)} %get-tuple-element.36), channel_id=1, source_target_pairs={{0,36},{4,32},{8,44},{12,40},{16,52},{20,48},{24,60},{28,56},{32,6... | collective-permute-start | bytes 5505032 | tf_op jit(solution)/shard_map/ppermute | solution.py:42
  788.4 229.6 %collective-permute-start.13 = (bf16[4,64,3584]{2,1,0:T(8,128)(2,1)}, bf16[4,64,3584]{2,1,0:T(8,128)(2,1)}, u32[]{:S(2)}, u32[]{:S(2)}) collective-permute-start(bf16[4,64,3584]{2,1,0:T(8,128)(2,1)} %get-tuple-element.27), channel_id=1, source_target_pairs={{0,8},{4,12},{8,16},{12,20},{16,24},{20,28},{24,0},{28,4},{32,40},... | collective-permute-start | bytes 5505032 | tf_op jit(solution)/shard_map/ppermute | solution.py:42
  1013.1 43.6 %collective-permute-start.16 = (bf16[4,64,3584]{2,1,0:T(8,128)(2,1)}, bf16[4,64,3584]{2,1,0:T(8,128)(2,1)S(1)}, u32[]{:S(2)}, u32[]{:S(2)}) collective-permute-start(bf16[4,64,3584]{2,1,0:T(8,128)(2,1)} %get-tuple-element.31), channel_id=1, source_target_pairs={{0,96},{4,100},{8,104},{12,108},{16,112},{20,116},{24,120},{28,124... | collective-permute-start | bytes 5505032 | tf_op jit(solution)/shard_map/ppermute | solution.py:42
  1013.2 43.5 %collective-permute-start.20 = (bf16[4,64,3584]{2,1,0:T(8,128)(2,1)}, bf16[4,64,3584]{2,1,0:T(8,128)(2,1)S(1)}, u32[]{:S(2)}, u32[]{:S(2)}) collective-permute-start(bf16[4,64,3584]{2,1,0:T(8,128)(2,1)} %get-tuple-element.35), channel_id=1, source_target_pairs={{0,32},{4,36},{8,40},{12,44},{16,48},{20,52},{24,56},{28,60},{32,6... | collective-permute-start | bytes 5505032 | tf_op jit(solution)/shard_map/ppermute | solution.py:42
  1016.2 42.7 %collective-permute-start.9 = (bf16[4,64,3584]{2,1,0:T(8,128)(2,1)}, bf16[4,64,3584]{2,1,0:T(8,128)(2,1)S(1)}, u32[]{:S(2)}, u32[]{:S(2)}) collective-permute-start(bf16[4,64,3584]{2,1,0:T(8,128)(2,1)} %get-tuple-element.23), channel_id=1, source_target_pairs={{0,24},{4,28},{8,0},{12,4},{16,8},{20,12},{24,16},{28,20},{32,56},... | collective-permute-start | bytes 5505032 | tf_op jit(solution)/shard_map/ppermute | solution.py:42
  1017.9 40.9 %collective-permute-start.15 = (bf16[4,64,3584]{2,1,0:T(8,128)(2,1)}, bf16[4,64,3584]{2,1,0:T(8,128)(2,1)}, u32[]{:S(2)}, u32[]{:S(2)}) collective-permute-start(bf16[4,64,3584]{2,1,0:T(8,128)(2,1)} %get-tuple-element.30), channel_id=1, source_target_pairs={{0,4},{4,0},{8,12},{12,8},{16,20},{20,16},{24,28},{28,24},{32,36},... | collective-permute-start | bytes 5505032 | tf_op jit(solution)/shard_map/ppermute | solution.py:42
  1017.9 40.9 %collective-permute-start.8 = (bf16[4,64,3584]{2,1,0:T(8,128)(2,1)}, bf16[4,64,3584]{2,1,0:T(8,128)(2,1)}, u32[]{:S(2)}, u32[]{:S(2)}) collective-permute-start(bf16[4,64,3584]{2,1,0:T(8,128)(2,1)} %get-tuple-element.22), channel_id=1, source_target_pairs={{0,4},{4,0},{8,12},{12,8},{16,20},{20,16},{24,28},{28,24},{32,36},... | collective-permute-start | bytes 5505032 | tf_op jit(solution)/shard_map/ppermute | solution.py:42
  (15 other events, 1318.8 us)

commit v2 on v1

--- a/solution.py
+++ b/solution.py
@@ -44,14 +44,13 @@
 
 def pick_kernel(targets, table, place, *refs):
     held = (refs[0:5], refs[5:10])
-    outs = refs[10:-1]
-    sem = refs[-1]
+    outs = refs[10:-3]
+    stage, sem, out_sem = refs[-3:]
     x, y, c = place[0], place[1], place[2]
     count = 0
     for side in range(2):
         own, before, after, low, high = held[side]
         for step, flip in targets:
-            out = outs[count // 4]
             for r in range(4):
                 if side == 0:
                     target = (x * NY + ((y + step) & 3)) * NC + (c ^ flip)
@@ -64,17 +63,20 @@
 
                     @pl.when(w < 2)
                     def _():
-                        pltpu.make_async_copy(low.at[jnp.minimum(w, 1)], out.at[r], sem.at[count]).start()
+                        pltpu.make_async_copy(low.at[jnp.minimum(w, 1)], stage.at[count], sem.at[count]).start()
 
                     @pl.when(w >= 2)
                     def _():
-                        pltpu.make_async_copy(high.at[jnp.maximum(w - 2, 0)], out.at[r], sem.at[count]).start()
+                        pltpu.make_async_copy(high.at[jnp.maximum(w - 2, 0)], stage.at[count], sem.at[count]).start()
                 else:
                     source = (own, after, None, before)[r]
-                    pltpu.make_async_copy(source.at[w], out.at[r], sem.at[count]).start()
+                    pltpu.make_async_copy(source.at[w], stage.at[count], sem.at[count]).start()
                 count += 1
     for i in range(count):
-        pltpu.make_async_copy(held[0][0].at[0], outs[i // 4].at[i % 4], sem.at[i]).wait()
+        pltpu.make_async_copy(held[0][0].at[0], stage.at[i], sem.at[i]).wait()
+        pltpu.make_async_copy(stage.at[i], outs[i // 4].at[i % 4], out_sem.at[i]).start()
+    for i in range(count):
+        pltpu.make_async_copy(stage.at[i], outs[i // 4].at[i % 4], out_sem.at[i]).wait()
 
 
 def pick(targets, table, place, held):
@@ -86,7 +88,12 @@
         out_shape=[shape] * sends,
         in_specs=[SMEM, SMEM] + [HBM] * 10,
         out_specs=[HBM] * sends,
-        scratch_shapes=[pltpu.SemaphoreType.DMA((sends * 4,))],
+        scratch_shapes=[
+            pltpu.VMEM((sends * 4, HR, WIDE), jnp.bfloat16),
+            pltpu.SemaphoreType.DMA((sends * 4,)),
+            pltpu.SemaphoreType.DMA((sends * 4,)),
+        ],
+        compiler_params=pltpu.CompilerParams(vmem_limit_bytes=12 * 1024 * 1024),
         cost_estimate=pl.CostEstimate(flops=0, bytes_accessed=2 * size, transcendentals=0),
     )(table, place, *held)
 
@@ -244,22 +251,24 @@
     own = [
         jnp.concatenate([tiles[:, s : s + HR], tile_labels[:, s : s + HR]], axis=2) for s in (0, HR)
     ]
-    held = []
-    for side in range(2):
-        dx, dy = ((1, 0), (0, 1))[side]
-        before = shift(own[side], dx, dy, 0)
-        after = shift(own[side], -dx, -dy, 0)
-        low = shift(before[:2], dx, dy, 0)
-        high = shift(after[2:], -dx, -dy, 0)
-        held += [own[side], before, after, low, high]
-
     identity = jnp.arange(home.shape[0], dtype=jnp.int32)
     storage = jnp.sum(jnp.where(candidates[:, :, None] == identity, home, 0), axis=2)
     owner = storage // (TILE_DEV * NZ)
     local = storage % TILE_DEV
     hit = owner.reshape(-1)[:, None] == jnp.arange(NDP, dtype=jnp.int32)[None, :]
     wanted = jnp.max(jnp.where(hit, local.reshape(-1)[:, None], 0), axis=0)
-    table = lax.all_gather(wanted, "dp")
+    asked = jnp.broadcast_to(wanted[None, :], (NDP, NDP))
+    table = lax.all_to_all(asked, "dp", split_axis=0, concat_axis=0, tiled=True)
+
+    held = []
+    for side in range(2):
+        dx, dy = ((1, 0), (0, 1))[side]
+        before = shift(own[side], dx, dy, 0)
+        after = shift(own[side], -dx, -dy, 0)
+        low, high, table = lax.optimization_barrier((before[:2], after[2:], table))
+        low = shift(low, dx, dy, 0)
+        high = shift(high, -dx, -dy, 0)
+        held += [own[side], before, after, low, high]
 
     parts = [embeddings]
     for r in range(1, NZ):

time: 1100 us -> 327 us (0.30)
  Pallas kernels: 928 us -> 63 us
  waiting for transfers between devices: 78.5 us -> 191 us
  blocking collectives: 20.4 us -> 0 us
    pallas_call x4, Pallas kernels: 898 us -> 29.9 us  [pick(): pl.pallas_call(functools.partial(pick_kernel, targets), out_shape=[shape]...]
    ppermute x22, waiting for transfers between devices: 78.5 us -> 166 us  [shift(): return lax.ppermute(value, 'dp', pairs)]
    ppermute x3, waiting for transfers between devices: 0.01 us -> 24.8 us  [body(): lax.ppermute(piece, 'mp', [(i, (i - r) % NZ) for i in range(NZ)])]
    unnamed x1 -> x0, blocking collectives: 20.4 us -> none
  transfers between devices with their start and end apart: 25 -> 26, of which waited for: 5 -> 13; matrix products, arithmetic and copies ran while one was open for 2% -> 5% of each run, Pallas kernels for 82% -> 9%
where the time goes in v2:
time: 327 us; the launch traced here: 321 us
  waiting for transfers between devices  191 us (58%)
  Pallas kernels  63 us (19%)
  starting transfers between devices  39.5 us (12%)
  local copies, waits for them, and re-layouts  24.1 us (7%)
    ppermute x22, waiting for transfers between devices, shift(): return lax.ppermute(value, 'dp', pairs)  166 us
    pallas_call x1, Pallas kernels, score(): pl.pallas_call(score_kernel, out_shape=jax.ShapeDtypeStruct((ROWS, LAB),...  33.1 us
    pallas_call x4, Pallas kernels, pick(): pl.pallas_call(functools.partial(pick_kernel, targets), out_shape=[shape]...  29.9 us
    ppermute x3, waiting for transfers between devices, body(): lax.ppermute(piece, 'mp', [(i, (i - r) % NZ) for i in range(NZ)])  24.8 us
    ppermute x22, starting transfers between devices, shift(): return lax.ppermute(value, 'dp', pairs)  23.2 us
    ppermute x3, starting transfers between devices, body(): lax.ppermute(piece, 'mp', [(i, (i - r) % NZ) for i in range(NZ)])  8.8 us
    all_to_all x1, starting transfers between devices, body(): table = lax.all_to_all(asked, 'dp', split_axis=0, concat_axis=0, tiled=True)  7.49 us
    unnamed x46, local copies, waits for them, and re-layouts  7.38 us
  transfers between devices with their start and end apart: 26, of which 13 were waited for; matrix products, arithmetic and copies ran while one was open for 5% of the time, Pallas kernels for 9%

profile of v2, /device:TPU:12, one launch (start us, length us, event | category | flops | bytes accessed | tf_op | source)
XLA Modules:
  0.0 321.2 jit_solution(2513187802414090620)
XLA Ops:
  7.8 6.8 %constant_dynamic-slice_fusion = (bf16[2048,640]{1,0:T(8,128)(2,1)}, bf16[2048,640]{1,0:T(8,128)(2,1)}, bf16[2048,640]{1,0:T(8,128)(2,1)}) fusion(bf16[8192,640]{1,0:T(8,128)(2,1)} %refs_16_.1, s32[]{:T(128)S(6)} %select_n.118, s32[]{:T(128)S(6)} %select_n.116, s32[]{:T(128)S(6)} %select_n.114), kind=kLoop, calls=%fused_computation.27 | loop fusion | bytes 15728652 | tf_op jit(solution)/shard_map/dynamic_slice | solution.py:276
  14.6 4.0 %collective-permute-start.22 = (bf16[2048,640]{1,0:T(8,128)(2,1)}, bf16[2048,640]{1,0:T(8,128)(2,1)}, u32[]{:S(2)}, u32[]{:S(2)}) collective-permute-start(bf16[2048,640]{1,0:T(8,128)(2,1)} %get-tuple-element.53), channel_id=1, source_target_pairs={{0,3},{1,0},{2,1},{3,2},{4,7},{5,4},{6,5},{7,6},{8,11},{9,8},{10,9... | collective-permute-start | bytes 7864328 | tf_op jit(solution)/shard_map/ppermute | solution.py:277
  18.9 25.3 %collective-permute-done.2.refs_1_ = bf16[4,64,3584]{2,1,0:T(8,128)(2,1)} collective-permute-done((bf16[4,64,3584]{2,1,0:T(8,128)(2,1)S(1)}, bf16[4,64,3584]{2,1,0:T(8,128)(2,1)}, u32[]{:S(2)}, u32[]{:S(2)}) %collective-permute-start.2) | collective-permute-done | bytes 1835040 | tf_op jit(solution)/shard_map/ppermute | solution.py:42
  44.2 3.9 %collective-permute-start.23 = (bf16[2048,640]{1,0:T(8,128)(2,1)}, bf16[2048,640]{1,0:T(8,128)(2,1)}, u32[]{:S(2)}, u32[]{:S(2)}) collective-permute-start(bf16[2048,640]{1,0:T(8,128)(2,1)} %get-tuple-element.52), channel_id=1, source_target_pairs={{0,2},{1,3},{2,0},{3,1},{4,6},{5,7},{6,4},{7,5},{8,10},{9,11},{10,... | collective-permute-start | bytes 7864328 | tf_op jit(solution)/shard_map/ppermute | solution.py:277
  49.4 7.5 %all-to-all-start = ((s32[32,1,32]{2,1,0:T(1,128)}), s32[32,1,32]{2,1,0:T(1,128)S(1)}, u32[]{:S(2)}, u32[]{:S(2)}) async-start(s32[32,1,32]{2,1,0:T(1,128)} %broadcast_in_dim.52), calls=%async_computation | async-start | bytes 32768 | tf_op jit(solution)/shard_map/all_to_all | solution.py:261
  56.8 2.2 slice.42
  59.0 2.2 slice.43
  67.2 19.1 %collective-permute-done.6.refs_8_ = bf16[2,64,3584]{2,1,0:T(8,128)(2,1)S(1)} collective-permute-done((bf16[2,64,3584]{2,1,0:T(8,128)(2,1)S(1)}, bf16[2,64,3584]{2,1,0:T(8,128)(2,1)S(1)}, u32[]{:S(2)}, u32[]{:S(2)}) %collective-permute-start.6) | collective-permute-done | bytes 917536 | tf_op jit(solution)/shard_map/ppermute | solution.py:42
  89.5 19.0 %collective-permute-done.5.refs_4_ = bf16[2,64,3584]{2,1,0:T(8,128)(2,1)} collective-permute-done((bf16[2,64,3584]{2,1,0:T(8,128)(2,1)}, bf16[2,64,3584]{2,1,0:T(8,128)(2,1)}, u32[]{:S(2)}, u32[]{:S(2)}) %collective-permute-start.5) | collective-permute-done | bytes 917536 | tf_op jit(solution)/shard_map/ppermute | solution.py:42
  109.6 7.5 %shard_map.67 = (bf16[4,64,3584]{2,1,0:T(8,128)(2,1)S(1)}, bf16[4,64,3584]{2,1,0:T(8,128)(2,1)S(1)}, bf16[4,64,3584]{2,1,0:T(8,128)(2,1)S(1)}, bf16[4,64,3584]{2,1,0:T(8,128)(2,1)S(1)}) custom-call(s32[32,32]{1,0:T(8,128)S(1)} %bitcast.7, s32[4]{0:T(128)S(1)} %pad_add_fusion.place, bf16[4,64,3584]{2,1,0:T(8,128)(2,1)S(1)} %pad_maximum_fusion.1.refs_0_, ...), custom_call_target="tpu_custom_call" | custom-call | bytes 14680064 | tf_op jit(solution)/shard_map/pallas_call | solution.py:86
  119.0 11.1 %collective-permute-done.22.refs_17_ = bf16[2048,640]{1,0:T(8,128)(2,1)} collective-permute-done((bf16[2048,640]{1,0:T(8,128)(2,1)}, bf16[2048,640]{1,0:T(8,128)(2,1)}, u32[]{:S(2)}, u32[]{:S(2)}) %collective-permute-start.22) | collective-permute-done | bytes 2621472 | tf_op jit(solution)/shard_map/ppermute | solution.py:277
  131.9 7.5 %shard_map.66 = (bf16[4,64,3584]{2,1,0:T(8,128)(2,1)S(1)}, bf16[4,64,3584]{2,1,0:T(8,128)(2,1)S(1)}, bf16[4,64,3584]{2,1,0:T(8,128)(2,1)S(1)}, bf16[4,64,3584]{2,1,0:T(8,128)(2,1)S(1)}) custom-call(s32[32,32]{1,0:T(8,128)S(1)} %bitcast.8, s32[4]{0:T(128)S(1)} %pad_add_fusion.place, bf16[4,64,3584]{2,1,0:T(8,128)(2,1)S(1)} %pad_maximum_fusion.1.refs_0_, ...), custom_call_target="tpu_custom_call" | custom-call | bytes 14680064 | tf_op jit(solution)/shard_map/pallas_call | solution.py:86
  139.4 7.5 %shard_map.65 = (bf16[4,64,3584]{2,1,0:T(8,128)(2,1)S(1)}, bf16[4,64,3584]{2,1,0:T(8,128)(2,1)S(1)}, bf16[4,64,3584]{2,1,0:T(8,128)(2,1)S(1)}, bf16[4,64,3584]{2,1,0:T(8,128)(2,1)S(1)}) custom-call(s32[32,32]{1,0:T(8,128)S(1)} %bitcast.9, s32[4]{0:T(128)S(1)} %pad_add_fusion.place, bf16[4,64,3584]{2,1,0:T(8,128)(2,1)S(1)} %pad_maximum_fusion.1.refs_0_, ...), custom_call_target="tpu_custom_call" | custom-call | bytes 14680064 | tf_op jit(solution)/shard_map/pallas_call | solution.py:86
  146.9 13.7 %collective-permute-done.24.refs_19_ = bf16[2048,640]{1,0:T(8,128)(2,1)} collective-permute-done((bf16[2048,640]{1,0:T(8,128)(2,1)}, bf16[2048,640]{1,0:T(8,128)(2,1)}, u32[]{:S(2)}, u32[]{:S(2)}) %collective-permute-start.24) | collective-permute-done | bytes 2621472 | tf_op jit(solution)/shard_map/ppermute | solution.py:277
  162.3 36.5 %collective-permute-done.12.refs_5_ = bf16[4,64,3584]{2,1,0:T(8,128)(2,1)S(1)} collective-permute-done((bf16[4,64,3584]{2,1,0:T(8,128)(2,1)S(1)}, bf16[4,64,3584]{2,1,0:T(8,128)(2,1)S(1)}, u32[]{:S(2)}, u32[]{:S(2)}) %collective-permute-start.12) | collective-permute-done | bytes 1835040 | tf_op jit(solution)/shard_map/ppermute | solution.py:42
  198.8 2.5 collective-permute-start.17
  204.2 7.5 %shard_map.64 = (bf16[4,64,3584]{2,1,0:T(8,128)(2,1)S(1)}, bf16[4,64,3584]{2,1,0:T(8,128)(2,1)S(1)}, bf16[4,64,3584]{2,1,0:T(8,128)(2,1)S(1)}, bf16[4,64,3584]{2,1,0:T(8,128)(2,1)S(1)}) custom-call(s32[32,32]{1,0:T(8,128)S(1)} %bitcast.10, s32[4]{0:T(128)S(1)} %pad_add_fusion.place, bf16[4,64,3584]{2,1,0:T(8,128)(2,1)S(1)} %pad_maximum_fusion.1.refs_0_, ...), custom_call_target="tpu_custom_call" | custom-call | bytes 14680064 | tf_op jit(solution)/shard_map/pallas_call | solution.py:86
  214.2 23.6 %collective-permute-done.10.refs_3_ = bf16[4,64,3584]{2,1,0:T(8,128)(2,1)S(1)} collective-permute-done((bf16[4,64,3584]{2,1,0:T(8,128)(2,1)S(1)}, bf16[4,64,3584]{2,1,0:T(8,128)(2,1)S(1)}, u32[]{:S(2)}, u32[]{:S(2)}) %collective-permute-start.10) | collective-permute-done | bytes 1835040 | tf_op jit(solution)/shard_map/ppermute | solution.py:42
  239.9 2.7 collective-permute-done.17.refs_11_
  242.6 2.8 collective-permute-start.9
  245.4 31.6 %collective-permute-done.13.refs_6_ = bf16[4,64,3584]{2,1,0:T(8,128)(2,1)} collective-permute-done((bf16[4,64,3584]{2,1,0:T(8,128)(2,1)S(1)}, bf16[4,64,3584]{2,1,0:T(8,128)(2,1)}, u32[]{:S(2)}, u32[]{:S(2)}) %collective-permute-start.13) | collective-permute-done | bytes 1835040 | tf_op jit(solution)/shard_map/ppermute | solution.py:42
  277.7 4.5 %collective-permute-done.16.refs_10_ = bf16[4,64,3584]{2,1,0:T(8,128)(2,1)S(1)} collective-permute-done((bf16[4,64,3584]{2,1,0:T(8,128)(2,1)S(1)}, bf16[4,64,3584]{2,1,0:T(8,128)(2,1)S(1)}, u32[]{:S(2)}, u32[]{:S(2)}) %collective-permute-start.16) | collective-permute-done | bytes 1835040 | tf_op jit(solution)/shard_map/ppermute | solution.py:42
  282.5 2.9 collective-permute-done.9.refs_2_
  288.0 33.1 %shard_map.68 = bf16[2048,1024]{1,0:T(8,128)(2,1)} custom-call(s32[64]{0:T(128)} %copy-done.6, s32[64]{0:T(128)} %and_convert_fusion.fresh, s32[8]{0:T(128)} %counts.1, s32[4]{0:T(128)} %copy-done.2, bf16[4,64,3584]{2,1,0:T(8,128)(2,1)} %copy-done.3, bf16[4,64,3584]{2,1,0:T(8,128)(2,1)} %copy-done.21, bf16[4,64,3584]{2,1,0:T(8,128)(2,1)} %copy-done.19, ...), custom_call_target="tpu_custom_call" | custom-call | flops 15032385536 | bytes 44040192 | tf_op jit(solution)/shard_map/pallas_call | solution.py:216
  (103 shorter events, 36.0 us)
Async XLA Ops:
  2.3 41.9 %collective-permute-start.2 = (bf16[4,64,3584]{2,1,0:T(8,128)(2,1)S(1)}, bf16[4,64,3584]{2,1,0:T(8,128)(2,1)}, u32[]{:S(2)}, u32[]{:S(2)}) collective-permute-start(bf16[4,64,3584]{2,1,0:T(8,128)(2,1)S(1)} %pad_maximum_fusion.1.refs_0_), channel_id=1, source_target_pairs={{0,32},{4,36},{8,40},{12,44},{16,48},{20,52},{24,56},{28,60},{32,6... | collective-permute-start | bytes 5505032 | tf_op jit(solution)/shard_map/ppermute | solution.py:42
  3.5 55.5 %collective-permute-start.3 = (bf16[4,64,3584]{2,1,0:T(8,128)(2,1)S(1)}, bf16[4,64,3584]{2,1,0:T(8,128)(2,1)}, u32[]{:S(2)}, u32[]{:S(2)}) collective-permute-start(bf16[4,64,3584]{2,1,0:T(8,128)(2,1)S(1)} %pad_maximum_fusion.1.refs_0_), channel_id=1, source_target_pairs={{0,96},{4,100},{8,104},{12,108},{16,112},{20,116},{24,120},{28,124... | collective-permute-start | bytes 5505032 | tf_op jit(solution)/shard_map/ppermute | solution.py:42
  5.8 55.5 %collective-permute-start = (bf16[4,64,3584]{2,1,0:T(8,128)(2,1)}, bf16[4,64,3584]{2,1,0:T(8,128)(2,1)}, u32[]{:S(2)}, u32[]{:S(2)}) collective-permute-start(bf16[4,64,3584]{2,1,0:T(8,128)(2,1)} %pad_maximum_fusion.refs_5_), channel_id=1, source_target_pairs={{0,8},{4,12},{8,16},{12,20},{16,24},{20,28},{24,0},{28,4},{32,40},... | collective-permute-start | bytes 5505032 | tf_op jit(solution)/shard_map/ppermute | solution.py:42
  7.4 55.1 %collective-permute-start.1 = (bf16[4,64,3584]{2,1,0:T(8,128)(2,1)}, bf16[4,64,3584]{2,1,0:T(8,128)(2,1)}, u32[]{:S(2)}, u32[]{:S(2)}) collective-permute-start(bf16[4,64,3584]{2,1,0:T(8,128)(2,1)} %pad_maximum_fusion.refs_5_), channel_id=1, source_target_pairs={{0,24},{4,28},{8,0},{12,4},{16,8},{20,12},{24,16},{28,20},{32,56},... | collective-permute-start | bytes 5505032 | tf_op jit(solution)/shard_map/ppermute | solution.py:42
  14.6 115.5 %collective-permute-start.22 = (bf16[2048,640]{1,0:T(8,128)(2,1)}, bf16[2048,640]{1,0:T(8,128)(2,1)}, u32[]{:S(2)}, u32[]{:S(2)}) collective-permute-start(bf16[2048,640]{1,0:T(8,128)(2,1)} %get-tuple-element.53), channel_id=1, source_target_pairs={{0,3},{1,0},{2,1},{3,2},{4,7},{5,4},{6,5},{7,6},{8,11},{9,8},{10,9... | collective-permute-start | bytes 7864328 | tf_op jit(solution)/shard_map/ppermute | solution.py:277
  44.2 87.7 %collective-permute-start.23 = (bf16[2048,640]{1,0:T(8,128)(2,1)}, bf16[2048,640]{1,0:T(8,128)(2,1)}, u32[]{:S(2)}, u32[]{:S(2)}) collective-permute-start(bf16[2048,640]{1,0:T(8,128)(2,1)} %get-tuple-element.52), channel_id=1, source_target_pairs={{0,2},{1,3},{2,0},{3,1},{4,6},{5,7},{6,4},{7,5},{8,10},{9,11},{10,... | collective-permute-start | bytes 7864328 | tf_op jit(solution)/shard_map/ppermute | solution.py:277
  63.7 22.6 %collective-permute-start.6 = (bf16[2,64,3584]{2,1,0:T(8,128)(2,1)S(1)}, bf16[2,64,3584]{2,1,0:T(8,128)(2,1)S(1)}, u32[]{:S(2)}, u32[]{:S(2)}) collective-permute-start(bf16[2,64,3584]{2,1,0:T(8,128)(2,1)S(1)} %slice.38), channel_id=1, source_target_pairs={{0,8},{4,12},{8,16},{12,20},{16,24},{20,28},{24,0},{28,4},{32,40},... | collective-permute-start | bytes 2752520 | tf_op jit(solution)/shard_map/ppermute | solution.py:42
  65.2 22.3 %collective-permute-start.7 = (bf16[2,64,3584]{2,1,0:T(8,128)(2,1)S(1)}, bf16[2,64,3584]{2,1,0:T(8,128)(2,1)S(1)}, u32[]{:S(2)}, u32[]{:S(2)}) collective-permute-start(bf16[2,64,3584]{2,1,0:T(8,128)(2,1)S(1)} %slice.39), channel_id=1, source_target_pairs={{0,24},{4,28},{8,0},{12,4},{16,8},{20,12},{24,16},{28,20},{32,56},... | collective-permute-start | bytes 2752520 | tf_op jit(solution)/shard_map/ppermute | solution.py:42
  65.8 23.6 %collective-permute-start.4 = (bf16[2,64,3584]{2,1,0:T(8,128)(2,1)}, bf16[2,64,3584]{2,1,0:T(8,128)(2,1)}, u32[]{:S(2)}, u32[]{:S(2)}) collective-permute-start(bf16[2,64,3584]{2,1,0:T(8,128)(2,1)} %slice.42), channel_id=1, source_target_pairs={{0,32},{4,36},{8,40},{12,44},{16,48},{20,52},{24,56},{28,60},{32,6... | collective-permute-start | bytes 2752520 | tf_op jit(solution)/shard_map/ppermute | solution.py:42
  86.3 22.1 %collective-permute-start.5 = (bf16[2,64,3584]{2,1,0:T(8,128)(2,1)}, bf16[2,64,3584]{2,1,0:T(8,128)(2,1)}, u32[]{:S(2)}, u32[]{:S(2)}) collective-permute-start(bf16[2,64,3584]{2,1,0:T(8,128)(2,1)} %slice.43), channel_id=1, source_target_pairs={{0,96},{4,100},{8,104},{12,108},{16,112},{20,116},{24,120},{28,124... | collective-permute-start | bytes 2752520 | tf_op jit(solution)/shard_map/ppermute | solution.py:42
  88.5 72.0 %collective-permute-start.24 = (bf16[2048,640]{1,0:T(8,128)(2,1)}, bf16[2048,640]{1,0:T(8,128)(2,1)}, u32[]{:S(2)}, u32[]{:S(2)}) collective-permute-start(bf16[2048,640]{1,0:T(8,128)(2,1)} %get-tuple-element.51), channel_id=1, source_target_pairs={{0,1},{1,2},{2,3},{3,0},{4,5},{5,6},{6,7},{7,4},{8,9},{9,10},{10,1... | collective-permute-start | bytes 7864328 | tf_op jit(solution)/shard_map/ppermute | solution.py:277
  117.1 44.5 %collective-permute-start.11 = (bf16[4,64,3584]{2,1,0:T(8,128)(2,1)S(1)}, bf16[4,64,3584]{2,1,0:T(8,128)(2,1)S(1)}, u32[]{:S(2)}, u32[]{:S(2)}) collective-permute-start(bf16[4,64,3584]{2,1,0:T(8,128)(2,1)S(1)} %get-tuple-element.37), channel_id=1, source_target_pairs={{0,16},{4,20},{8,24},{12,28},{16,0},{20,4},{24,8},{28,12},{32,48},... | collective-permute-start | bytes 5505032 | tf_op jit(solution)/shard_map/ppermute | solution.py:42
  119.0 79.8 %collective-permute-start.12 = (bf16[4,64,3584]{2,1,0:T(8,128)(2,1)S(1)}, bf16[4,64,3584]{2,1,0:T(8,128)(2,1)S(1)}, u32[]{:S(2)}, u32[]{:S(2)}) collective-permute-start(bf16[4,64,3584]{2,1,0:T(8,128)(2,1)S(1)} %get-tuple-element.38), channel_id=1, source_target_pairs={{0,20},{4,16},{8,28},{12,24},{16,4},{20,0},{24,12},{28,8},{32,52},... | collective-permute-start | bytes 5505032 | tf_op jit(solution)/shard_map/ppermute | solution.py:42
  130.1 71.2 %collective-permute-start.18 = (bf16[4,64,3584]{2,1,0:T(8,128)(2,1)S(1)}, bf16[4,64,3584]{2,1,0:T(8,128)(2,1)S(1)}, u32[]{:S(2)}, u32[]{:S(2)}) collective-permute-start(bf16[4,64,3584]{2,1,0:T(8,128)(2,1)S(1)} %get-tuple-element.45), channel_id=1, source_target_pairs={{0,64},{4,68},{8,72},{12,76},{16,80},{20,84},{24,88},{28,92},{32,9... | collective-permute-start | bytes 5505032 | tf_op jit(solution)/shard_map/ppermute | solution.py:42
  131.9 70.6 %collective-permute-start.19 = (bf16[4,64,3584]{2,1,0:T(8,128)(2,1)S(1)}, bf16[4,64,3584]{2,1,0:T(8,128)(2,1)S(1)}, u32[]{:S(2)}, u32[]{:S(2)}) collective-permute-start(bf16[4,64,3584]{2,1,0:T(8,128)(2,1)S(1)} %get-tuple-element.46), channel_id=1, source_target_pairs={{0,68},{4,64},{8,76},{12,72},{16,84},{20,80},{24,92},{28,88},{32,1... | collective-permute-start | bytes 5505032 | tf_op jit(solution)/shard_map/ppermute | solution.py:42
  160.5 77.3 %collective-permute-start.10 = (bf16[4,64,3584]{2,1,0:T(8,128)(2,1)S(1)}, bf16[4,64,3584]{2,1,0:T(8,128)(2,1)S(1)}, u32[]{:S(2)}, u32[]{:S(2)}) collective-permute-start(bf16[4,64,3584]{2,1,0:T(8,128)(2,1)S(1)} %get-tuple-element.36), channel_id=1, source_target_pairs={{0,28},{4,24},{8,4},{12,0},{16,12},{20,8},{24,20},{28,16},{32,60},... | collective-permute-start | bytes 5505032 | tf_op jit(solution)/shard_map/ppermute | solution.py:42
  161.6 76.8 %collective-permute-start.14 = (bf16[4,64,3584]{2,1,0:T(8,128)(2,1)S(1)}, bf16[4,64,3584]{2,1,0:T(8,128)(2,1)S(1)}, u32[]{:S(2)}, u32[]{:S(2)}) collective-permute-start(bf16[4,64,3584]{2,1,0:T(8,128)(2,1)S(1)} %get-tuple-element.40), channel_id=1, source_target_pairs={{0,12},{4,8},{8,20},{12,16},{16,28},{20,24},{24,4},{28,0},{32,44},... | collective-permute-start | bytes 5505032 | tf_op jit(solution)/shard_map/ppermute | solution.py:42
  198.8 43.8 %collective-permute-start.17 = (bf16[4,64,3584]{2,1,0:T(8,128)(2,1)S(1)}, bf16[4,64,3584]{2,1,0:T(8,128)(2,1)S(1)}, u32[]{:S(2)}, u32[]{:S(2)}) collective-permute-start(bf16[4,64,3584]{2,1,0:T(8,128)(2,1)S(1)} %get-tuple-element.44), channel_id=1, source_target_pairs={{0,100},{4,96},{8,108},{12,104},{16,116},{20,112},{24,124},{28,120... | collective-permute-start | bytes 5505032 | tf_op jit(solution)/shard_map/ppermute | solution.py:42
  201.3 44.1 %collective-permute-start.21 = (bf16[4,64,3584]{2,1,0:T(8,128)(2,1)S(1)}, bf16[4,64,3584]{2,1,0:T(8,128)(2,1)S(1)}, u32[]{:S(2)}, u32[]{:S(2)}) collective-permute-start(bf16[4,64,3584]{2,1,0:T(8,128)(2,1)S(1)} %get-tuple-element.48), channel_id=1, source_target_pairs={{0,36},{4,32},{8,44},{12,40},{16,52},{20,48},{24,60},{28,56},{32,6... | collective-permute-start | bytes 5505032 | tf_op jit(solution)/shard_map/ppermute | solution.py:42
  202.5 74.5 %collective-permute-start.13 = (bf16[4,64,3584]{2,1,0:T(8,128)(2,1)S(1)}, bf16[4,64,3584]{2,1,0:T(8,128)(2,1)}, u32[]{:S(2)}, u32[]{:S(2)}) collective-permute-start(bf16[4,64,3584]{2,1,0:T(8,128)(2,1)S(1)} %get-tuple-element.39), channel_id=1, source_target_pairs={{0,8},{4,12},{8,16},{12,20},{16,24},{20,28},{24,0},{28,4},{32,40},... | collective-permute-start | bytes 5505032 | tf_op jit(solution)/shard_map/ppermute | solution.py:42
  237.9 44.4 %collective-permute-start.16 = (bf16[4,64,3584]{2,1,0:T(8,128)(2,1)S(1)}, bf16[4,64,3584]{2,1,0:T(8,128)(2,1)S(1)}, u32[]{:S(2)}, u32[]{:S(2)}) collective-permute-start(bf16[4,64,3584]{2,1,0:T(8,128)(2,1)S(1)} %get-tuple-element.43), channel_id=1, source_target_pairs={{0,96},{4,100},{8,104},{12,108},{16,112},{20,116},{24,120},{28,124... | collective-permute-start | bytes 5505032 | tf_op jit(solution)/shard_map/ppermute | solution.py:42
  238.5 44.0 %collective-permute-start.20 = (bf16[4,64,3584]{2,1,0:T(8,128)(2,1)S(1)}, bf16[4,64,3584]{2,1,0:T(8,128)(2,1)S(1)}, u32[]{:S(2)}, u32[]{:S(2)}) collective-permute-start(bf16[4,64,3584]{2,1,0:T(8,128)(2,1)S(1)} %get-tuple-element.47), channel_id=1, source_target_pairs={{0,32},{4,36},{8,40},{12,44},{16,48},{20,52},{24,56},{28,60},{32,6... | collective-permute-start | bytes 5505032 | tf_op jit(solution)/shard_map/ppermute | solution.py:42
  242.6 42.7 %collective-permute-start.9 = (bf16[4,64,3584]{2,1,0:T(8,128)(2,1)S(1)}, bf16[4,64,3584]{2,1,0:T(8,128)(2,1)S(1)}, u32[]{:S(2)}, u32[]{:S(2)}) collective-permute-start(bf16[4,64,3584]{2,1,0:T(8,128)(2,1)S(1)} %get-tuple-element.35), channel_id=1, source_target_pairs={{0,24},{4,28},{8,0},{12,4},{16,8},{20,12},{24,16},{28,20},{32,56},... | collective-permute-start | bytes 5505032 | tf_op jit(solution)/shard_map/ppermute | solution.py:42
  245.4 40.0 %collective-permute-start.15 = (bf16[4,64,3584]{2,1,0:T(8,128)(2,1)S(1)}, bf16[4,64,3584]{2,1,0:T(8,128)(2,1)S(1)}, u32[]{:S(2)}, u32[]{:S(2)}) collective-permute-start(bf16[4,64,3584]{2,1,0:T(8,128)(2,1)S(1)} %get-tuple-element.42), channel_id=1, source_target_pairs={{0,4},{4,0},{8,12},{12,8},{16,20},{20,16},{24,28},{28,24},{32,36},... | collective-permute-start | bytes 5505032 | tf_op jit(solution)/shard_map/ppermute | solution.py:42
  (25 other events, 706.4 us)

commit v3 on v0

v3 whole, which is shorter than its diff:
```python
import functools
import math

import jax
import jax.numpy as jnp
from jax import lax
from jax.experimental import pallas as pl
from jax.experimental.pallas import tpu as pltpu
from jax.sharding import PartitionSpec as P

D = 2560
LAB = 1024
TR = 128
HR = TR // 2
BR = 256
CAND = 8
NX = 4
NY = 4
NC = 2
NZ = 4
NDP = NX * NY * NC
TILE_DEV = 4
BLK_DEV = 8
PIECE = D // NZ
ROWS = BLK_DEV * BR
WIDE = D + LAB
NOTE = 128
MIB = 1024 * 1024
HBM = pl.BlockSpec(memory_space=pl.ANY)
SMEM = pl.BlockSpec(memory_space=pltpu.SMEM)


def dp_index(x, y, c):
    return ((x % NX) * NY + (y % NY)) * NC + c


def shift(value, dx, dy, flip):
    pairs = [
        (dp_index(x, y, c), dp_index(x + dx, y + dy, c ^ flip))
        for x in range(NX)
        for y in range(NY)
        for c in range(NC)
    ]
    return lax.ppermute(value, "dp", pairs)


class Lanes:
    def __init__(self):
        self.last = {}

    def send(self, value, dx, dy, flip=0):
        axis, step = ("x", dx % 4) if dx else ("y", dy % 4)
        lanes = [(axis, 1), (axis, 3)] if step == 2 else [(axis, step)]
        ends = [self.last[lane] for lane in lanes if lane in self.last]
        if ends:
            value, *_ = lax.optimization_barrier((value, *ends))
        out = shift(value, dx, dy, flip)
        if step != 2:
            self.last[lanes[0]] = out
        return out


def pick_kernel(jobs, which, table, place, *refs):
    outs = refs[-3 - len(jobs) : -3]
    stage, sem, out_sem = refs[-3:]
    x, y, c = place[0], place[1], place[2]
    moves = []
    for job, (side, step, flip, left, width) in enumerate(jobs):
        own, before, after, far = (refs[side * 8 + 2 * i : side * 8 + 2 * i + 2] for i in range(4))
        for r in which:
            if side == 0:
                owner = (((x + r) & 3) * NY + y) * NC + c
            else:
                owner = (x * NY + ((y + r) & 3)) * NC + c
            row = side * 2 + flip if step == 2 else side * 8 + step * 2 + flip
            w = table[row, owner]
            source = (own, after, far, before)[r]
            at = len(moves)
            room = stage.at[at, :, pl.ds(0, width)]
            columns = pl.ds(left, width)

            @pl.when(w < 2)
            def _():
                piece = source[0].at[jnp.minimum(w, 1), :, columns]
                pltpu.make_async_copy(piece, room, sem.at[at]).start()

            @pl.when(w >= 2)
            def _():
                piece = source[1].at[jnp.maximum(w - 2, 0), :, columns]
                pltpu.make_async_copy(piece, room, sem.at[at]).start()

            moves.append((room, own[0].at[0, :, columns], outs[job].at[which.index(r)]))
    for i, (room, piece, out) in enumerate(moves):
        pltpu.make_async_copy(piece, room, sem.at[i]).wait()
        pltpu.make_async_copy(room, out, out_sem.at[i]).start()
    for i, (room, piece, out) in enumerate(moves):
        pltpu.make_async_copy(room, out, out_sem.at[i]).wait()


def pick(jobs, table, place, held, which=(0, 1, 2, 3)):
    number = len(jobs) * len(which)
    widest = max(job[4] for job in jobs)
    return pl.pallas_call(
        functools.partial(pick_kernel, jobs, which),
        out_shape=[jax.ShapeDtypeStruct((len(which), HR, job[4]), jnp.bfloat16) for job in jobs],
        in_specs=[SMEM, SMEM] + [HBM] * len(held),
        out_specs=[HBM] * len(jobs),
        scratch_shapes=[
            pltpu.VMEM((number, HR, widest), jnp.bfloat16),
            pltpu.SemaphoreType.DMA((number,)),
            pltpu.SemaphoreType.DMA((number,)),
        ],
        compiler_params=pltpu.CompilerParams(vmem_limit_bytes=60 * MIB),
        cost_estimate=pl.CostEstimate(
            flops=0,
            bytes_accessed=sum(4 * len(which) * HR * job[4] for job in jobs),
            transcendentals=0,
        ),
    )(table, place, *held)


def half_copies(got, place, o, start):
    x, y, c = place[0], place[1], place[2]
    rx = ((o >> 3) - x) & 3
    ry = ((o >> 1) - y) & 3
    rc = (o & 1) ^ c
    for side, near, r in ((0, ry, rx), (1, rx, ry)):
        which = near * 2 + rc
        for k in range(8):
            if k in (2, 6):

                @pl.when((which == k) & (r != 2))
                def _():
                    start(side, got[side][k], jnp.where(r == 3, 2, r))

                @pl.when((which == k) & (r == 2))
                def _():
                    start(side, got[side][8 + k // 4], 0)
            else:

                @pl.when(which == k)
                def _():
                    start(side, got[side][k], r)


def probs_kernel(owners, counts, place, *refs):
    got = (refs[0:10], refs[10:20])
    features = refs[20]
    out = refs[-5]
    cents, rows, tile_sem, row_sem = refs[-4:]
    step = pl.program_id(0)

    def row_copies(at):
        slot = lax.rem(at, 2)
        for r in range(NZ):
            start = pl.multiple_of(r * ROWS + at * BR, BR)
            yield pltpu.make_async_copy(
                features.at[pl.ds(start, BR), :],
                rows.at[slot, :, pl.ds(r * PIECE, PIECE)],
                row_sem.at[slot, r],
            )

    def tile_copy(at, j, side, ref, r):
        slot = lax.rem(at, 2)
        return pltpu.make_async_copy(
            ref.at[r, :, pl.ds(0, D)], cents.at[slot, j, pl.ds(side * HR, HR), :], tile_sem.at[slot, j, side]
        )

    def fetch(at):
        for copy in row_copies(at):
            copy.start()

        def one(j, carry):
            @pl.when(j < counts[at])
            def _():
                o = owners[at * CAND + j]
                half_copies(
                    got, place, o, lambda side, ref, r: tile_copy(at, j, side, ref, r).start()
                )

            return carry

        lax.fori_loop(0, CAND, one, 0)

    @pl.when(step == 0)
    def _():
        fetch(step)

    @pl.when(step + 1 < BLK_DEV)
    def _():
        fetch(step + 1)

    live = counts[step]
    for copy in row_copies(step):
        copy.wait()
    for j in range(CAND):

        @pl.when(j < live)
        def _():
            for side in range(2):
                tile_copy(step, j, side, got[side][0], 0).wait()

    slot = lax.rem(step, 2)
    scale = 2.0 / math.sqrt(D)

    def attend(slots):
        tiles = cents[slot, 0:slots].reshape(slots * TR, D)
        value = lax.dot_general(
            rows[slot], tiles, (((1,), (1,)), ((), ())), preferred_element_type=jnp.float32
        )
        column = lax.broadcasted_iota(jnp.int32, (BR, slots * TR), 1)
        value = jnp.where(column < live * TR, value * scale, -jnp.inf)
        peak = jnp.max(value, axis=1, keepdims=True)
        weights = jnp.exp(value - peak)
        total = jnp.sum(weights, axis=1, keepdims=True)
        out[:, 0 : slots * TR] = (weights / total).astype(jnp.bfloat16)
        if slots < CAND:
            out[:, slots * TR :] = jnp.zeros((BR, (CAND - slots) * TR), jnp.bfloat16)

    @pl.when(live <= 4)
    def _():
        attend(4)

    @pl.when((live > 4) & (live <= 6))
    def _():
        attend(6)

    @pl.when(live > 6)
    def _():
        attend(8)


def probabilities(owners, counts, place, got, features):
    return pl.pallas_call(
        probs_kernel,
        out_shape=jax.ShapeDtypeStruct((ROWS, CAND * TR), jnp.bfloat16),
        grid_spec=pltpu.PrefetchScalarGridSpec(
            num_scalar_prefetch=3,
            grid=(BLK_DEV,),
            in_specs=[HBM] * 21,
            out_specs=pl.BlockSpec((BR, CAND * TR), lambda s, *_: (s, 0)),
            scratch_shapes=[
                pltpu.VMEM((2, CAND, TR, D), jnp.bfloat16),
                pltpu.VMEM((2, BR, D), jnp.bfloat16),
                pltpu.SemaphoreType.DMA((2, CAND, 2)),
                pltpu.SemaphoreType.DMA((2, NZ)),
            ],
        ),
        compiler_params=pltpu.CompilerParams(
            dimension_semantics=("arbitrary",), vmem_limit_bytes=60 * MIB
        ),
        cost_estimate=pl.CostEstimate(
            flops=2 * ROWS * CAND * TR * D,
            bytes_accessed=(BLK_DEV * CAND * TR * D + ROWS * D) * 2,
            transcendentals=ROWS * CAND * TR,
        ),
    )(owners, counts, place, *got, features)


def mix_kernel(owners, counts, place, *refs):
    got = (refs[0:10], refs[10:20])
    probs, out, labs, sem = refs[20:]
    b = pl.program_id(0)

    def tile_copy(at, j, side, ref, r):
        slot = lax.rem(at, 2)
        left = ref.shape[2] - LAB
        rows = pl.ds(pl.multiple_of(j * TR + side * HR, HR), HR)
        return pltpu.make_async_copy(
            ref.at[r, :, pl.ds(left, LAB)], labs.at[slot, rows, :], sem.at[slot, j, side]
        )

    def used(at):
        return ((counts[at] + 1) // 2) * 2

    def fetch(at):
        def one(j, carry):
            o = owners[at * CAND + j]
            half_copies(
                got, place, o, lambda side, ref, r: tile_copy(at, j, side, ref, r).start()
            )
            return carry

        lax.fori_loop(0, used(at), one, 0)

    @pl.when(b == 0)
    def _():
        fetch(b)

    @pl.when(b + 1 < BLK_DEV)
    def _():
        fetch(b + 1)

    slots_used = used(b)
    for j in range(CAND):

        @pl.when(j < slots_used)
        def _():
            for side in range(2):
                tile_copy(b, j, side, got[side][0], 0).wait()

    slot = lax.rem(b, 2)

    def mix(slots):
        value = jnp.dot(
            probs[:, 0 : slots * TR], labs[slot, 0 : slots * TR], preferred_element_type=jnp.float32
        )
        out[...] = value.astype(jnp.bfloat16)

    for slots in (4, 6, 8):

        @pl.when(slots_used == slots)
        def _():
            mix(slots)


def mixture(owners, counts, place, got, probs):
    return pl.pallas_call(
        mix_kernel,
        out_shape=jax.ShapeDtypeStruct((ROWS, LAB), jnp.bfloat16),
        grid_spec=pltpu.PrefetchScalarGridSpec(
            num_scalar_prefetch=3,
            grid=(BLK_DEV,),
            in_specs=[HBM] * 20 + [pl.BlockSpec((BR, CAND * TR), lambda b, *_: (b, 0))],
            out_specs=pl.BlockSpec((BR, LAB), lambda b, *_: (b, 0)),
            scratch_shapes=[
                pltpu.VMEM((2, CAND * TR, LAB), jnp.bfloat16),
                pltpu.SemaphoreType.DMA((2, CAND, 2)),
            ],
        ),
        compiler_params=pltpu.CompilerParams(
            dimension_semantics=("arbitrary",), vmem_limit_bytes=60 * MIB
        ),
        cost_estimate=pl.CostEstimate(
            flops=2 * ROWS * CAND * TR * LAB,
            bytes_accessed=(BLK_DEV * CAND * TR * LAB + 2 * ROWS * LAB) * 2,
            transcendentals=0,
        ),
    )(owners, counts, place, *got, probs)


def jobs_of(step, left=0, width=WIDE, flips=(0, 1)):
    return tuple((side, s, flip, left, width) for flip in flips for side in range(2) for s in step)


NEAR = jobs_of((1, 3), flips=(0,))
CROSS = jobs_of((1, 3), flips=(1,))
HOME = jobs_of((0,))
FAR = jobs_of((2,), 0, D)
FAR_LABELS = jobs_of((2,), D, LAB)


def body(embeddings, centroids, labels, candidates, counts, home):
    me = lax.axis_index("dp")
    z = lax.axis_index("mp")
    place = jnp.stack([me // (NY * NC), (me // NC) % NY, me % NC, z]).astype(jnp.int32)
    line = Lanes()

    features = lax.all_to_all(embeddings, "mp", split_axis=0, concat_axis=0, tiled=True)

    identity = jnp.arange(home.shape[0], dtype=jnp.int32)
    storage = jnp.sum(jnp.where(candidates[:, :, None] == identity, home, 0), axis=2)
    owner = storage // (TILE_DEV * NZ)
    local = storage % TILE_DEV
    hit = owner.reshape(-1)[:, None] == jnp.arange(NDP, dtype=jnp.int32)[None, :]
    wanted = jnp.max(jnp.where(hit, local.reshape(-1)[:, None], 0), axis=0)
    note = jnp.pad(wanted, (0, NOTE - NDP)).astype(jnp.bfloat16)
    note = jnp.broadcast_to(note, (2, HR, NOTE))

    tiles = centroids.reshape(TILE_DEV, TR, D)
    tile_labels = labels.reshape(TILE_DEV, TR, LAB)
    ways = ((1, 0), (0, 1))
    own = [
        [
            jnp.concatenate(
                [a[t : t + 2, s * HR : (s + 1) * HR] for a in (tiles, tile_labels)] + [note], axis=2
            )
            for t in (0, 2)
        ]
        for s in range(2)
    ]
    before, after, far = ([[None, None] for _ in range(2)] for _ in range(3))
    for s, (dx, dy) in enumerate(ways):
        before[s][0] = line.send(own[s][0], dx, dy)
        after[s][1] = line.send(own[s][1], -dx, -dy)
    for s, (dx, dy) in enumerate(ways):
        before[s][1] = line.send(own[s][1], dx, dy)
        after[s][0] = line.send(own[s][0], -dx, -dy)

    def read(piece):
        return piece[0, 0, WIDE : WIDE + NDP].astype(jnp.int32)

    def swap(wishes):
        return lax.ppermute(wishes, "dp", [(i, i ^ 1) for i in range(NDP)])

    blank = jnp.zeros((NDP,), jnp.int32)
    near = [[wanted, read(after[1 - s][1]), blank, read(before[1 - s][0])] for s in range(2)]
    table = jnp.stack([row for s in range(2) for v in near[s] for row in (v, blank)])
    crossed = swap(jnp.stack(near[0] + near[1]))

    for s, (dx, dy) in enumerate(ways):
        far[s][0] = line.send(before[s][0], dx, dy)
        far[s][1] = line.send(after[s][1], -dx, -dy)

    def exchange(jobs, sends, got):
        for (side, step, flip, _, _), value in zip(jobs, sends, strict=True):
            if (step, flip) != (0, 0):
                value = line.send(value, step * side, step * (1 - side), flip)
            got[side][((-step) % 4) * 2 + flip] = value

    got = [[None] * 10, [None] * 10]
    held = [h for s in range(2) for h in own[s] + before[s] + after[s] + own[s]]
    exchange(NEAR, pick(NEAR, table, place, held, (0, 1, 3)), got)
    held = [h for s in range(2) for h in own[s] + before[s] + after[s] + far[s]]
    rest = pick(NEAR, table, place, held, (2,))
    crossed, *rest = lax.optimization_barrier((crossed, *rest))
    crossed = jnp.repeat(crossed, 2, axis=0)
    odd = (jnp.arange(16, dtype=jnp.int32) % 2 == 1)[:, None]
    sends = pick(CROSS + HOME, jnp.where(odd, crossed, table), place, held)
    distant = jnp.stack([read(far[1][0]), read(far[0][0])])
    distant = jnp.stack([distant, swap(distant)], axis=1).reshape(4, NDP)
    later = pick(FAR + FAR_LABELS, distant, place, held)
    rest[-1], sends, later = lax.optimization_barrier((rest[-1], sends, later))
    for (side, step, flip, _, _), value in zip(NEAR, rest, strict=True):
        got[side][9 - step // 2] = line.send(value, step * side, step * (1 - side), flip)
    exchange(CROSS + HOME, sends, got)
    exchange(FAR, later[: len(FAR)], got)
    got_labels = [list(g) for g in got]
    later, *_ = lax.optimization_barrier((later[len(FAR) :], got[0][4], got[0][5], got[1][4], got[1][5]))
    exchange(FAR_LABELS, later, got_labels)

    live = jnp.arange(CAND, dtype=jnp.int32)[None, :] < counts[:, None]
    slots = jnp.where(live, owner, owner[:, :1])
    flat = slots.reshape(-1)
    probs = probabilities(flat, counts, place, got[0] + got[1], features)
    return mixture(flat, counts, place, got_labels[0] + got_labels[1], probs)


def solution(mesh):
    placed = (
        P("dp", "mp"),
        P(("dp", "mp"), None),
        P(("dp", "mp"), None),
        P(("dp", "mp"), None),
        P(("dp", "mp")),
        P(),
    )
    return jax.shard_map(
        body, mesh=mesh, in_specs=placed, out_specs=P(("dp", "mp"), None), check_vma=False
    )
```

time: 812 us -> 282 us (0.35)
  the two profiles are of different devices: /device:TPU:12 before, /device:TPU:1 now
where the time goes in v3:
time: 282 us; the launch traced here: 281 us
  waiting for transfers between devices  143 us (51%)
  Pallas kernels  62 us (22%)
  starting transfers between devices  60.6 us (21%)
  other arithmetic  7.97 us (3%)
  local copies, waits for them, and re-layouts  6.82 us (2%)
    ppermute x34, waiting for transfers between devices, shift(): return lax.ppermute(value, 'dp', pairs)  143 us
    ppermute x34, starting transfers between devices, shift(): return lax.ppermute(value, 'dp', pairs)  49.7 us
    pallas_call x4, Pallas kernels, pick(): pl.pallas_call(functools.partial(pick_kernel, jobs, which), out_shape=[ja...  27.5 us
    pallas_call x1, Pallas kernels, probabilities(): pl.pallas_call(probs_kernel, out_shape=jax.ShapeDtypeStruct((ROWS, CAND *...  21.5 us
    pallas_call x1, Pallas kernels, mixture(): pl.pallas_call(mix_kernel, out_shape=jax.ShapeDtypeStruct((ROWS, LAB), jn...  13 us
    all_to_all x1, starting transfers between devices, body(): lax.all_to_all(embeddings, 'mp', split_axis=0, concat_axis=0, tiled=True)  5.98 us
  transfers between devices with their start and end apart: 37, of which 11 were waited for; matrix products, arithmetic and copies ran while one was open for 3% of the time, Pallas kernels for 17%

profile of v3, /device:TPU:1, one launch (start us, length us, event | category | flops | bytes accessed | tf_op | source)
XLA Modules:
  0.0 280.5 jit_solution(10346046933984247156)
XLA Ops:
  13.9 6.0 %all-to-all-start = ((bf16[4,2048,640]{2,1,0:T(8,128)(2,1)}), bf16[4,2048,640]{2,1,0:T(8,128)(2,1)}, u32[]{:S(2)}, u32[]{:S(2)}) async-start(bf16[4,2048,640]{2,1,0:T(8,128)(2,1)} %bitcast.38), calls=%async_computation | async-start | bytes 20971520 | tf_op jit(solution)/shard_map/all_to_all | solution.py:359
  19.9 11.5 %collective-permute-done.3.refs_2_ = bf16[2,64,3712]{2,1,0:T(8,128)(2,1)} collective-permute-done((bf16[2,64,3712]{2,1,0:T(8,128)(2,1)S(1)}, bf16[2,64,3712]{2,1,0:T(8,128)(2,1)}, u32[]{:S(2)}, u32[]{:S(2)}) %collective-permute-start.3) | collective-permute-done | bytes 950304 | tf_op jit(solution)/shard_map/ppermute | solution.py:44
  37.2 16.3 %collective-permute-done.5.refs_3_ = bf16[2,64,3712]{2,1,0:T(8,128)(2,1)} collective-permute-done((bf16[2,64,3712]{2,1,0:T(8,128)(2,1)S(1)}, bf16[2,64,3712]{2,1,0:T(8,128)(2,1)}, u32[]{:S(2)}, u32[]{:S(2)}) %collective-permute-start.5) | collective-permute-done | bytes 950304 | tf_op jit(solution)/shard_map/ppermute | solution.py:44
  64.0 5.8 %shard_map.67 = (bf16[3,64,3584]{2,1,0:T(8,128)(2,1)}, bf16[3,64,3584]{2,1,0:T(8,128)(2,1)}, bf16[3,64,3584]{2,1,0:T(8,128)(2,1)}, bf16[3,64,3584]{2,1,0:T(8,128)(2,1)}) custom-call(s32[16,32]{1,0:T(8,128)} %stack.59.table, s32[4]{0:T(128)} %pad_add_fusion.1.place, bf16[2,64,3712]{2,1,0:T(8,128)(2,1)} %copy-done, bf16[2,64,3712]{2,1,0:T(8,128)(2,1)} %copy-done.2, ...), custom_call_target="tpu_custom_call" | custom-call | bytes 11010048 | tf_op jit(solution)/shard_map/pallas_call | solution.py:103
  69.9 7.7 %collective-permute-done.12.refs_15_ = bf16[2,64,3712]{2,1,0:T(8,128)(2,1)S(1)} collective-permute-done((bf16[2,64,3712]{2,1,0:T(8,128)(2,1)}, bf16[2,64,3712]{2,1,0:T(8,128)(2,1)S(1)}, u32[]{:S(2)}, u32[]{:S(2)}) %collective-permute-start.12) | collective-permute-done | bytes 950304 | tf_op jit(solution)/shard_map/ppermute | solution.py:44
  77.6 3.0 %collective-permute-start.15 = (bf16[3,64,3584]{2,1,0:T(8,128)(2,1)}, bf16[3,64,3584]{2,1,0:T(8,128)(2,1)}, u32[]{:S(2)}, u32[]{:S(2)}) collective-permute-start(bf16[3,64,3584]{2,1,0:T(8,128)(2,1)} %get-tuple-element.117), channel_id=1, source_target_pairs={{0,24},{4,28},{8,0},{12,4},{16,8},{20,12},{24,16},{28,20},{32,56},... | collective-permute-start | bytes 4128776 | tf_op jit(solution)/shard_map/ppermute | solution.py:44
  83.4 4.8 %collective-permute-start.4 = (s32[8,32]{1,0:T(8,128)S(1)}, s32[8,32]{1,0:T(8,128)S(1)}, u32[]{:S(2)}, u32[]{:S(2)}) collective-permute-start(s32[8,32]{1,0:T(8,128)S(1)} %stack.58), channel_id=1, source_target_pairs={{0,4},{4,0},{8,12},{12,8},{16,20},{20,16},{24,28},{28,24},{32,36},... | collective-permute-start | bytes 3080 | tf_op jit(solution)/shard_map/ppermute | solution.py:394
  88.1 3.2 %shard_map.64 = (bf16[1,64,3584]{2,1,0:T(8,128)(2,1)}, bf16[1,64,3584]{2,1,0:T(8,128)(2,1)}, bf16[1,64,3584]{2,1,0:T(8,128)(2,1)}, bf16[1,64,3584]{2,1,0:T(8,128)(2,1)}) custom-call(s32[16,32]{1,0:T(8,128)} %stack.59.table, s32[4]{0:T(128)} %pad_add_fusion.1.place, bf16[2,64,3712]{2,1,0:T(8,128)(2,1)} %copy-done, bf16[2,64,3712]{2,1,0:T(8,128)(2,1)} %copy-done.2, ...), custom_call_target="tpu_custom_call" | custom-call | bytes 3670016 | tf_op jit(solution)/shard_map/pallas_call | solution.py:103
  93.5 11.6 %shard_map.65 = (bf16[4,64,3584]{2,1,0:T(8,128)(2,1)}, bf16[4,64,3584]{2,1,0:T(8,128)(2,1)}, bf16[4,64,3584]{2,1,0:T(8,128)(2,1)}, bf16[4,64,3584]{2,1,0:T(8,128...) custom-call(s32[16,32]{1,0:T(8,128)} %broadcast_select_fusion.table,, ...), custom_call_target="tpu_custom_call" | custom-call | bytes 29360128 | tf_op jit(solution)/shard_map/pallas_call | solution.py:103
  105.7 6.9 %shard_map.66 = (bf16[4,64,2560]{2,1,0:T(8,128)(2,1)}, bf16[4,64,2560]{2,1,0:T(8,128)(2,1)}, bf16[4,64,2560]{2,1,0:T(8,128)(2,1)}, bf16[4,64,2560]{2,1,0:T(8,128...) custom-call(s32[4,32]{1,0:T(4,128)} %bitcast.42, ...), custom_call_target="tpu_custom_call" | custom-call | bytes 14680064 | tf_op jit(solution)/shard_map/pallas_call | solution.py:103
  118.9 7.4 %collective-permute-done.16.refs_8_ = bf16[1,64,3584]{2,1,0:T(8,128)(2,1)S(1)} collective-permute-done((bf16[1,64,3584]{2,1,0:T(8,128)(2,1)}, bf16[1,64,3584]{2,1,0:T(8,128)(2,1)S(1)}, u32[]{:S(2)}, u32[]{:S(2)}) %collective-permute-start.16) | collective-permute-done | bytes 458784 | tf_op jit(solution)/shard_map/ppermute | solution.py:44
  126.3 4.1 %collective-permute-start.17 = (bf16[4,64,3584]{2,1,0:T(8,128)(2,1)}, bf16[4,64,3584]{2,1,0:T(8,128)(2,1)}, u32[]{:S(2)}, u32[]{:S(2)}) collective-permute-start(bf16[4,64,3584]{2,1,0:T(8,128)(2,1)} %get-tuple-element.121), channel_id=1, source_target_pairs={{0,28},{4,24},{8,4},{12,0},{16,12},{20,8},{24,20},{28,16},{32,60},... | collective-permute-start | bytes 5505032 | tf_op jit(solution)/shard_map/ppermute | solution.py:44
  130.5 3.0 %collective-permute-start.28 = (bf16[4,64,3584]{2,1,0:T(8,128)(2,1)}, bf16[4,64,3584]{2,1,0:T(8,128)(2,1)}, u32[]{:S(2)}, u32[]{:S(2)}) collective-permute-start(bf16[4,64,3584]{2,1,0:T(8,128)(2,1)} %get-tuple-element.148), channel_id=1, source_target_pairs={{0,100},{4,96},{8,108},{12,104},{16,116},{20,112},{24,124},{28,120... | collective-permute-start | bytes 5505032 | tf_op jit(solution)/shard_map/ppermute | solution.py:44
  133.6 36.8 %collective-permute-done.17.refs_3_ = bf16[4,64,3584]{2,1,0:T(8,128)(2,1)} collective-permute-done((bf16[4,64,3584]{2,1,0:T(8,128)(2,1)}, bf16[4,64,3584]{2,1,0:T(8,128)(2,1)}, u32[]{:S(2)}, u32[]{:S(2)}) %collective-permute-start.17) | collective-permute-done | bytes 1835040 | tf_op jit(solution)/shard_map/ppermute | solution.py:44
  170.4 3.2 %collective-permute-done.20.refs_7_ = bf16[4,64,3584]{2,1,0:T(8,128)(2,1)} collective-permute-done((bf16[4,64,3584]{2,1,0:T(8,128)(2,1)}, bf16[4,64,3584]{2,1,0:T(8,128)(2,1)}, u32[]{:S(2)}, u32[]{:S(2)}) %collective-permute-start.20) | collective-permute-done | bytes 1835040 | tf_op jit(solution)/shard_map/ppermute | solution.py:44
  173.6 3.3 %collective-permute-start.22 = (bf16[4,64,2560]{2,1,0:T(8,128)(2,1)}, bf16[4,64,2560]{2,1,0:T(8,128)(2,1)}, u32[]{:S(2)}, u32[]{:S(2)}) collective-permute-start(bf16[4,64,2560]{2,1,0:T(8,128)(2,1)} %get-tuple-element.135), channel_id=1, source_target_pairs={{0,20},{4,16},{8,28},{12,24},{16,4},{20,0},{24,12},{28,8},{32,52},... | collective-permute-start | bytes 3932168 | tf_op jit(solution)/shard_map/ppermute | solution.py:44
  176.9 3.2 %collective-permute-start.30 = (bf16[4,64,2560]{2,1,0:T(8,128)(2,1)}, bf16[4,64,2560]{2,1,0:T(8,128)(2,1)}, u32[]{:S(2)}, u32[]{:S(2)}) collective-permute-start(bf16[4,64,2560]{2,1,0:T(8,128)(2,1)} %get-tuple-element.151), channel_id=1, source_target_pairs={{0,68},{4,64},{8,76},{12,72},{16,84},{20,80},{24,92},{28,88},{32,1... | collective-permute-start | bytes 3932168 | tf_op jit(solution)/shard_map/ppermute | solution.py:44
  180.1 25.5 %collective-permute-done.21.refs_4_ = bf16[4,64,2560]{2,1,0:T(8,128)(2,1)} collective-permute-done((bf16[4,64,2560]{2,1,0:T(8,128)(2,1)}, bf16[4,64,2560]{2,1,0:T(8,128)(2,1)}, u32[]{:S(2)}, u32[]{:S(2)}) %collective-permute-start.21) | collective-permute-done | bytes 1310752 | tf_op jit(solution)/shard_map/ppermute | solution.py:44
  205.7 28.7 %collective-permute-done.22.refs_5_ = bf16[4,64,2560]{2,1,0:T(8,128)(2,1)} collective-permute-done((bf16[4,64,2560]{2,1,0:T(8,128)(2,1)}, bf16[4,64,2560]{2,1,0:T(8,128)(2,1)}, u32[]{:S(2)}, u32[]{:S(2)}) %collective-permute-start.22) | collective-permute-done | bytes 1310752 | tf_op jit(solution)/shard_map/ppermute | solution.py:44
  234.3 3.0 %collective-permute-done.30.refs_15_ = bf16[4,64,2560]{2,1,0:T(8,128)(2,1)} collective-permute-done((bf16[4,64,2560]{2,1,0:T(8,128)(2,1)}, bf16[4,64,2560]{2,1,0:T(8,128)(2,1)}, u32[]{:S(2)}, u32[]{:S(2)}) %collective-permute-start.30) | collective-permute-done | bytes 1310752 | tf_op jit(solution)/shard_map/ppermute | solution.py:44
  237.3 3.4 %collective-permute-start.32 = (bf16[4,64,1024]{2,1,0:T(8,128)(2,1)}, bf16[4,64,1024]{2,1,0:T(8,128)(2,1)}, u32[]{:S(2)}, u32[]{:S(2)}) collective-permute-start(bf16[4,64,1024]{2,1,0:T(8,128)(2,1)} %get-tuple-element.155), channel_id=1, source_target_pairs={{0,20},{4,16},{8,28},{12,24},{16,4},{20,0},{24,12},{28,8},{32,52},... | collective-permute-start | bytes 1572872 | tf_op jit(solution)/shard_map/ppermute | solution.py:44
  240.9 2.9 %collective-permute-start.35 = (bf16[4,64,1024]{2,1,0:T(8,128)(2,1)}, bf16[4,64,1024]{2,1,0:T(8,128)(2,1)}, u32[]{:S(2)}, u32[]{:S(2)}) collective-permute-start(bf16[4,64,1024]{2,1,0:T(8,128)(2,1)} %get-tuple-element.162), channel_id=1, source_target_pairs={{0,68},{4,64},{8,76},{12,72},{16,84},{20,80},{24,92},{28,88},{32,1... | collective-permute-start | bytes 1572872 | tf_op jit(solution)/shard_map/ppermute | solution.py:44
  243.9 21.5 %shard_map.68.refs_20_ = bf16[2048,1024]{1,0:T(8,128)(2,1)} custom-call(s32[64]{0:T(128)} %get-tuple-element.163.owners, s32[8]{0:T(128)} %counts.3, s32[4]{0:T(128)} %pad_add_fusion.1.place, bf16[4,64,3584]{2,1,0:T(8,128)(2,1)} %get-tuple-element.114.refs_0_, bf16[4,64,3584]{2,1,0:T(8,128)(2,1)} %copy-done.6, ...), custom_call_target="tpu_custom_call" | custom-call | flops 10737418240 | bytes 52428800 | tf_op jit(solution)/shard_map/pallas_call | solution.py:234
  267.4 13.0 %shard_map.69 = bf16[2048,1024]{1,0:T(8,128)(2,1)} custom-call(s32[64]{0:T(128)} %get-tuple-element.163.owners, s32[8]{0:T(128)} %counts.3, s32[4]{0:T(128)} %pad_add_fusion.1.place, bf16[4,64,3584]{2,1,0:T(8,128)(2,1)} %get-tuple-element.114.refs_0_, bf16[4,64,3584]{2,1,0:T(8,128)(2,1)} %copy-done.6, bf16[3,64,3584]{2,1,0:T(8,128)(2,1)} %collective-permute-done.15.refs_2_, ...), custom_call_target="tpu_custom_call" | custom-call | flops 4294967296 | bytes 25165824 | tf_op jit(solution)/shard_map/pallas_call | solution.py:318
  (114 shorter events, 44.3 us)
Async XLA Ops:
  7.6 23.7 %collective-permute-start.3 = (bf16[2,64,3712]{2,1,0:T(8,128)(2,1)S(1)}, bf16[2,64,3712]{2,1,0:T(8,128)(2,1)}, u32[]{:S(2)}, u32[]{:S(2)}) collective-permute-start(bf16[2,64,3712]{2,1,0:T(8,128)(2,1)S(1)} %get-tuple-element.85.refs_0_.refs_6_), channel_id=1, source_target_pairs={{0,32},{4,36},{8,40},{12,44},{16,48},{20,52},{24,56},{28,60},{32,6... | collective-permute-start | bytes 2850824 | tf_op jit(solution)/shard_map/ppermute | solution.py:44
  11.0 23.0 %collective-permute-start.1 = (bf16[2,64,3712]{2,1,0:T(8,128)(2,1)S(1)}, bf16[2,64,3712]{2,1,0:T(8,128)(2,1)}, u32[]{:S(2)}, u32[]{:S(2)}) collective-permute-start(bf16[2,64,3712]{2,1,0:T(8,128)(2,1)S(1)} %get-tuple-element.89.refs_8_.refs_14_), channel_id=1, source_target_pairs={{0,8},{4,12},{8,16},{12,20},{16,24},{20,28},{24,0},{28,4},{32,40},... | collective-permute-start | bytes 2850824 | tf_op jit(solution)/shard_map/ppermute | solution.py:44
  12.4 23.3 %collective-permute-start = (bf16[2,64,3712]{2,1,0:T(8,128)(2,1)}, bf16[2,64,3712]{2,1,0:T(8,128)(2,1)}, u32[]{:S(2)}, u32[]{:S(2)}) collective-permute-start(bf16[2,64,3712]{2,1,0:T(8,128)(2,1)} %get-tuple-element.88.refs_9_.refs_15_), channel_id=1, source_target_pairs={{0,24},{4,28},{8,0},{12,4},{16,8},{20,12},{24,16},{28,20},{32,56},... | collective-permute-start | bytes 2850824 | tf_op jit(solution)/shard_map/ppermute | solution.py:44
  13.9 230.0 %all-to-all-start = ((bf16[4,2048,640]{2,1,0:T(8,128)(2,1)}), bf16[4,2048,640]{2,1,0:T(8,128)(2,1)}, u32[]{:S(2)}, u32[]{:S(2)}) async-start(bf16[4,2048,640]{2,1,0:T(8,128)(2,1)} %bitcast.38), calls=%async_computation | async-start | bytes 20971520 | tf_op jit(solution)/shard_map/all_to_all | solution.py:359
  53.6 27.0 %collective-permute-start.7 = (bf16[2,64,3712]{2,1,0:T(8,128)(2,1)}, bf16[2,64,3712]{2,1,0:T(8,128)(2,1)S(1)}, u32[]{:S(2)}, u32[]{:S(2)}) collective-permute-start(bf16[2,64,3712]{2,1,0:T(8,128)(2,1)} %collective-permute-done.3.refs_2_), channel_id=1, source_target_pairs={{0,32},{4,36},{8,40},{12,44},{16,48},{20,52},{24,56},{28,60},{32,6... | collective-permute-start | bytes 2850824 | tf_op jit(solution)/shard_map/ppermute | solution.py:44
  53.6 27.1 %collective-permute-start.8 = (bf16[2,64,3712]{2,1,0:T(8,128)(2,1)}, bf16[2,64,3712]{2,1,0:T(8,128)(2,1)S(1)}, u32[]{:S(2)}, u32[]{:S(2)}) collective-permute-start(bf16[2,64,3712]{2,1,0:T(8,128)(2,1)} %collective-permute-done.2.refs_5_), channel_id=1, source_target_pairs={{0,96},{4,100},{8,104},{12,108},{16,112},{20,116},{24,120},{28,124... | collective-permute-start | bytes 2850824 | tf_op jit(solution)/shard_map/ppermute | solution.py:44
  56.7 23.9 %collective-permute-start.11 = (bf16[2,64,3712]{2,1,0:T(8,128)(2,1)}, bf16[2,64,3712]{2,1,0:T(8,128)(2,1)}, u32[]{:S(2)}, u32[]{:S(2)}) collective-permute-start(bf16[2,64,3712]{2,1,0:T(8,128)(2,1)} %collective-permute-done.1.refs_10_), channel_id=1, source_target_pairs={{0,8},{4,12},{8,16},{12,20},{16,24},{20,28},{24,0},{28,4},{32,40},... | collective-permute-start | bytes 2850824 | tf_op jit(solution)/shard_map/ppermute | solution.py:44
  77.6 35.7 %collective-permute-start.15 = (bf16[3,64,3584]{2,1,0:T(8,128)(2,1)}, bf16[3,64,3584]{2,1,0:T(8,128)(2,1)}, u32[]{:S(2)}, u32[]{:S(2)}) collective-permute-start(bf16[3,64,3584]{2,1,0:T(8,128)(2,1)} %get-tuple-element.117), channel_id=1, source_target_pairs={{0,24},{4,28},{8,0},{12,4},{16,8},{20,12},{24,16},{28,20},{32,56},... | collective-permute-start | bytes 4128776 | tf_op jit(solution)/shard_map/ppermute | solution.py:44
  80.6 35.5 %collective-permute-start.18 = (bf16[3,64,3584]{2,1,0:T(8,128)(2,1)}, bf16[3,64,3584]{2,1,0:T(8,128)(2,1)}, u32[]{:S(2)}, u32[]{:S(2)}) collective-permute-start(bf16[3,64,3584]{2,1,0:T(8,128)(2,1)} %get-tuple-element.130), channel_id=1, source_target_pairs={{0,8},{4,12},{8,16},{12,20},{16,24},{20,28},{24,0},{28,4},{32,40},... | collective-permute-start | bytes 4128776 | tf_op jit(solution)/shard_map/ppermute | solution.py:44
  80.6 35.5 %collective-permute-start.23 = (bf16[3,64,3584]{2,1,0:T(8,128)(2,1)}, bf16[3,64,3584]{2,1,0:T(8,128)(2,1)}, u32[]{:S(2)}, u32[]{:S(2)}) collective-permute-start(bf16[3,64,3584]{2,1,0:T(8,128)(2,1)} %get-tuple-element.140), channel_id=1, source_target_pairs={{0,32},{4,36},{8,40},{12,44},{16,48},{20,52},{24,56},{28,60},{32,6... | collective-permute-start | bytes 4128776 | tf_op jit(solution)/shard_map/ppermute | solution.py:44
  80.7 35.5 %collective-permute-start.26 = (bf16[3,64,3584]{2,1,0:T(8,128)(2,1)}, bf16[3,64,3584]{2,1,0:T(8,128)(2,1)}, u32[]{:S(2)}, u32[]{:S(2)}) collective-permute-start(bf16[3,64,3584]{2,1,0:T(8,128)(2,1)} %get-tuple-element.146), channel_id=1, source_target_pairs={{0,96},{4,100},{8,104},{12,108},{16,112},{20,116},{24,120},{28,124... | collective-permute-start | bytes 4128776 | tf_op jit(solution)/shard_map/ppermute | solution.py:44
  126.3 44.1 %collective-permute-start.17 = (bf16[4,64,3584]{2,1,0:T(8,128)(2,1)}, bf16[4,64,3584]{2,1,0:T(8,128)(2,1)}, u32[]{:S(2)}, u32[]{:S(2)}) collective-permute-start(bf16[4,64,3584]{2,1,0:T(8,128)(2,1)} %get-tuple-element.121), channel_id=1, source_target_pairs={{0,28},{4,24},{8,4},{12,0},{16,12},{20,8},{24,20},{28,16},{32,60},... | collective-permute-start | bytes 5505032 | tf_op jit(solution)/shard_map/ppermute | solution.py:44
  130.3 43.3 %collective-permute-start.20 = (bf16[4,64,3584]{2,1,0:T(8,128)(2,1)}, bf16[4,64,3584]{2,1,0:T(8,128)(2,1)}, u32[]{:S(2)}, u32[]{:S(2)}) collective-permute-start(bf16[4,64,3584]{2,1,0:T(8,128)(2,1)} %get-tuple-element.132), channel_id=1, source_target_pairs={{0,12},{4,8},{8,20},{12,16},{16,28},{20,24},{24,4},{28,0},{32,44},... | collective-permute-start | bytes 5505032 | tf_op jit(solution)/shard_map/ppermute | solution.py:44
  130.4 46.5 %collective-permute-start.25 = (bf16[4,64,3584]{2,1,0:T(8,128)(2,1)}, bf16[4,64,3584]{2,1,0:T(8,128)(2,1)}, u32[]{:S(2)}, u32[]{:S(2)}) collective-permute-start(bf16[4,64,3584]{2,1,0:T(8,128)(2,1)} %get-tuple-element.142), channel_id=1, source_target_pairs={{0,36},{4,32},{8,44},{12,40},{16,52},{20,48},{24,60},{28,56},{32,6... | collective-permute-start | bytes 5505032 | tf_op jit(solution)/shard_map/ppermute | solution.py:44
  130.5 46.4 %collective-permute-start.28 = (bf16[4,64,3584]{2,1,0:T(8,128)(2,1)}, bf16[4,64,3584]{2,1,0:T(8,128)(2,1)}, u32[]{:S(2)}, u32[]{:S(2)}) collective-permute-start(bf16[4,64,3584]{2,1,0:T(8,128)(2,1)} %get-tuple-element.148), channel_id=1, source_target_pairs={{0,100},{4,96},{8,108},{12,104},{16,116},{20,112},{24,124},{28,120... | collective-permute-start | bytes 5505032 | tf_op jit(solution)/shard_map/ppermute | solution.py:44
  133.4 110.4 %collective-permute-start.33 = (bf16[4,64,3584]{2,1,0:T(8,128)(2,1)}, bf16[4,64,3584]{2,1,0:T(8,128)(2,1)}, u32[]{:S(2)}, u32[]{:S(2)}) collective-permute-start(bf16[4,64,3584]{2,1,0:T(8,128)(2,1)} %get-tuple-element.158), channel_id=1, source_target_pairs={{0,4},{4,0},{8,12},{12,8},{16,20},{20,16},{24,28},{28,24},{32,36},... | collective-permute-start | bytes 5505032 | tf_op jit(solution)/shard_map/ppermute | solution.py:44
  173.6 32.0 %collective-permute-start.21 = (bf16[4,64,2560]{2,1,0:T(8,128)(2,1)}, bf16[4,64,2560]{2,1,0:T(8,128)(2,1)}, u32[]{:S(2)}, u32[]{:S(2)}) collective-permute-start(bf16[4,64,2560]{2,1,0:T(8,128)(2,1)} %get-tuple-element.133), channel_id=1, source_target_pairs={{0,16},{4,20},{8,24},{12,28},{16,0},{20,4},{24,8},{28,12},{32,48},... | collective-permute-start | bytes 3932168 | tf_op jit(solution)/shard_map/ppermute | solution.py:44
  173.6 60.7 %collective-permute-start.22 = (bf16[4,64,2560]{2,1,0:T(8,128)(2,1)}, bf16[4,64,2560]{2,1,0:T(8,128)(2,1)}, u32[]{:S(2)}, u32[]{:S(2)}) collective-permute-start(bf16[4,64,2560]{2,1,0:T(8,128)(2,1)} %get-tuple-element.135), channel_id=1, source_target_pairs={{0,20},{4,16},{8,28},{12,24},{16,4},{20,0},{24,12},{28,8},{32,52},... | collective-permute-start | bytes 3932168 | tf_op jit(solution)/shard_map/ppermute | solution.py:44
  176.9 57.4 %collective-permute-start.29 = (bf16[4,64,2560]{2,1,0:T(8,128)(2,1)}, bf16[4,64,2560]{2,1,0:T(8,128)(2,1)}, u32[]{:S(2)}, u32[]{:S(2)}) collective-permute-start(bf16[4,64,2560]{2,1,0:T(8,128)(2,1)} %get-tuple-element.149), channel_id=1, source_target_pairs={{0,64},{4,68},{8,72},{12,76},{16,80},{20,84},{24,88},{28,92},{32,9... | collective-permute-start | bytes 3932168 | tf_op jit(solution)/shard_map/ppermute | solution.py:44
  176.9 60.4 %collective-permute-start.30 = (bf16[4,64,2560]{2,1,0:T(8,128)(2,1)}, bf16[4,64,2560]{2,1,0:T(8,128)(2,1)}, u32[]{:S(2)}, u32[]{:S(2)}) collective-permute-start(bf16[4,64,2560]{2,1,0:T(8,128)(2,1)} %get-tuple-element.151), channel_id=1, source_target_pairs={{0,68},{4,64},{8,76},{12,72},{16,84},{20,80},{24,92},{28,88},{32,1... | collective-permute-start | bytes 3932168 | tf_op jit(solution)/shard_map/ppermute | solution.py:44
  237.3 28.1 %collective-permute-start.31 = (bf16[4,64,1024]{2,1,0:T(8,128)(2,1)}, bf16[4,64,1024]{2,1,0:T(8,128)(2,1)}, u32[]{:S(2)}, u32[]{:S(2)}) collective-permute-start(bf16[4,64,1024]{2,1,0:T(8,128)(2,1)} %get-tuple-element.153), channel_id=1, source_target_pairs={{0,16},{4,20},{8,24},{12,28},{16,0},{20,4},{24,8},{28,12},{32,48},... | collective-permute-start | bytes 1572872 | tf_op jit(solution)/shard_map/ppermute | solution.py:44
  237.3 28.1 %collective-permute-start.32 = (bf16[4,64,1024]{2,1,0:T(8,128)(2,1)}, bf16[4,64,1024]{2,1,0:T(8,128)(2,1)}, u32[]{:S(2)}, u32[]{:S(2)}) collective-permute-start(bf16[4,64,1024]{2,1,0:T(8,128)(2,1)} %get-tuple-element.155), channel_id=1, source_target_pairs={{0,20},{4,16},{8,28},{12,24},{16,4},{20,0},{24,12},{28,8},{32,52},... | collective-permute-start | bytes 1572872 | tf_op jit(solution)/shard_map/ppermute | solution.py:44
  240.7 24.7 %collective-permute-start.34 = (bf16[4,64,1024]{2,1,0:T(8,128)(2,1)}, bf16[4,64,1024]{2,1,0:T(8,128)(2,1)}, u32[]{:S(2)}, u32[]{:S(2)}) collective-permute-start(bf16[4,64,1024]{2,1,0:T(8,128)(2,1)} %get-tuple-element.160), channel_id=1, source_target_pairs={{0,64},{4,68},{8,72},{12,76},{16,80},{20,84},{24,88},{28,92},{32,9... | collective-permute-start | bytes 1572872 | tf_op jit(solution)/shard_map/ppermute | solution.py:44
  240.9 26.5 %collective-permute-start.35 = (bf16[4,64,1024]{2,1,0:T(8,128)(2,1)}, bf16[4,64,1024]{2,1,0:T(8,128)(2,1)}, u32[]{:S(2)}, u32[]{:S(2)}) collective-permute-start(bf16[4,64,1024]{2,1,0:T(8,128)(2,1)} %get-tuple-element.162), channel_id=1, source_target_pairs={{0,68},{4,64},{8,76},{12,72},{16,84},{20,80},{24,92},{28,88},{32,1... | collective-permute-start | bytes 1572872 | tf_op jit(solution)/shard_map/ppermute | solution.py:44
  (26 other events, 802.1 us)
